TPU v7x, 768 devices: a whole 4x8x12 slice. The times are simulated.
768 devices in a mesh: px: 64 (over x, y, core), py: 12 (over z).
Axes of the slice: x: 4, y: 8, z: 12, core: 2. Of those that a mesh axis runs over, the one named last changes fastest.
Arguments:
- fields: float32 [6, 35, 786432], P(None, None, ('px', 'py')), may hold values from -6 to 6
- metric: float32 [3, 3, 786432], P(None, None, ('px', 'py')), may hold values from -6 to 6
- normals: float32 [3, 4, 786432], P(None, None, ('px', 'py')), may hold values from -1 to 1
- face_scale: float32 [4, 786432], P(None, ('px', 'py')), may hold values from 0.5 to 3
- permittivity: float32 [786432], P(('px', 'py')), may hold values from 1 to 8
- derivative: float32 [3, 35, 35], replicated, may hold values from -1 to 1
- face_interp: float32 [4, 15, 35], replicated, may hold values from -1 to 1
- lift: float32 [35, 60], replicated, may hold values from -0.75 to 0.75
- neighbor: int32 [64, 12, 4096], P('px', 'py'), may hold values from 0 to 4607, as said below
- levels: int32 [64, 12, 8], replicated, may hold values from 0 to 1, as said below
Outputs:
- rate: float32 [6, 35, 786432], P(None, None, ('px', 'py'))
Inputs may be any that keep to these rules, and one draw needn't show every extreme that they name: `neighbor`: on every subdomain each code below 4096 pairs two distinct slots mutually; each code 4 * 1024 + d * 128 + j (d < 4, j < 128) appears exactly once on every subdomain, on a slot of an element of block j // 16. `levels`: at most 4 ones among the 8 blocks of one subdomain, reached on some subdomain.
All inputs are finite; a program needn't handle non-finite values.
Results may differ from a plain program's by a relative error of at most 0.0003.
Values sent between devices are 32-bit elements; how exact they have to be, the bound alone decides.
No kernel may reach another device: no remote copies, remote signals or barrier semaphores. Data moves between devices by JAX's collectives and lax.ppermute only.
A program may use at most 128 MiB of HBM per device.

v0:
```python
import jax
import jax.numpy as jnp
from jax import lax
from jax.experimental import pallas as pl
from jax.experimental.pallas import tpu as pltpu
from jax.sharding import PartitionSpec as P

F32 = jnp.float32
BF16 = jnp.bfloat16
BLK = 128
BFB = 16
NB = 8
NF = 4
NP = 35
NPAD = 40
KPAD = 48
FPAD = 16
STEP = 0.05
SLOTS = 4 * NB * BLK
FSLOTS = 4 * NF * BLK
FRECV = 4 * NF * BFB
ZROW = FSLOTS + FRECV
TAB = SLOTS + 4 * NB * BFB
FTAB = ZROW + 8
VMEM_LIMIT = 48 * 1024 * 1024


def split(x):
    hi = x.astype(BF16)
    lo = (x - hi.astype(F32)).astype(BF16)
    return hi, lo


def node_products(matrix, nodal):
    pad = jnp.zeros((KPAD - NPAD, 6 * BLK), F32)
    wide = jnp.concatenate([jnp.concatenate(nodal, axis=1), pad], axis=0)
    hi, lo = split(wide)
    return jnp.dot(matrix, jnp.concatenate([hi, lo, hi], axis=0), preferred_element_type=F32)


def store_traces(products, table, stride, base):
    for f in range(4):
        rows = products[f * FPAD : (f + 1) * FPAD]
        parts = [rows[:, c * BLK : (c + 1) * BLK] for c in range(6)]
        tile = jnp.concatenate(parts + [jnp.zeros((BLK - 6 * FPAD, BLK), F32)], axis=0)
        table[pl.ds(f * stride + base, BLK), :] = tile.T


def curls(products, metric, lanes):
    def nodal(a, c):
        return products[64 + a * NPAD : 64 + (a + 1) * NPAD, c * BLK : (c + 1) * BLK]

    rows = [[metric[i, a : a + 1, lanes] for a in range(3)] for i in range(3)]

    def grad(i, c):
        return rows[i][0] * nodal(0, c) + rows[i][1] * nodal(1, c) + rows[i][2] * nodal(2, c)

    curl_h = [grad(1, 5) - grad(2, 4), grad(2, 3) - grad(0, 5), grad(0, 4) - grad(1, 3)]
    curl_e = [grad(1, 2) - grad(2, 1), grad(2, 0) - grad(0, 2), grad(0, 1) - grad(1, 0)]
    return curl_h + curl_e


def cross(n, v):
    return [n[1] * v[2] - n[2] * v[1], n[2] * v[0] - n[0] * v[2], n[0] * v[1] - n[1] * v[0]]


def lifted_flux(outer, table, stride, base, normals, scale, lanes, lift):
    faces = [[], [], [], [], [], []]
    for f in range(4):
        at = pl.ds(f * stride + base, BLK)
        jump = (outer[at, :] - table[at, :]).T
        de = [jump[c * FPAD : (c + 1) * FPAD] for c in range(3)]
        dh = [jump[c * FPAD : (c + 1) * FPAD] for c in range(3, 6)]
        n = [normals[i, f : f + 1, lanes] for i in range(3)]
        half = 0.5 * scale[f : f + 1, lanes]
        dot_e = n[0] * de[0] + n[1] * de[1] + n[2] * de[2]
        dot_h = n[0] * dh[0] + n[1] * dh[1] + n[2] * dh[2]
        nh = cross(n, dh)
        ne = cross(n, de)
        for i in range(3):
            faces[i].append((nh[i] + de[i] - dot_e * n[i]) * half)
            faces[3 + i].append((dh[i] - dot_h * n[i] - ne[i]) * half)
    wide = jnp.concatenate([jnp.concatenate(x, axis=0) for x in faces], axis=1)
    hi, lo = split(wide)
    out = jnp.dot(lift, jnp.concatenate([hi, lo, hi], axis=0), preferred_element_type=F32)
    return [out[:NPAD, c * BLK : (c + 1) * BLK] for c in range(6)]


def tendency(curl, lifted, medium, lanes):
    inverse = 1.0 / medium[:, lanes]
    electric = [(curl[c] + lifted[c]) * inverse for c in range(3)]
    return electric + [lifted[c] - curl[c] for c in range(3, 6)]


def copy_rows(index, source, target, count, unroll):
    def body(g, _):
        base = pl.multiple_of(g * unroll, unroll)
        for r in range(unroll):
            target[pl.ds(base + r, 1), :] = source[pl.ds(index[base + r], 1), :]
        return 0

    lax.fori_loop(0, count // unroll, body, 0)


def send_rows(index, table, outs, width):
    for d in range(4):
        def body(g, _, d=d):
            base = pl.multiple_of(g * 16, 16)
            for r in range(16):
                outs[d][pl.ds(base + r, 1), :] = table[pl.ds(index[d * width + base + r], 1), :]
            return 0

        lax.fori_loop(0, width // 16, body, 0)


def pad_nodes(fields, padded):
    for c in range(6):
        padded[c, 32:NPAD, :] = jnp.zeros((NPAD - 32, NB * BLK), F32)
        padded[c, 0:NP, :] = fields[c]


def block_lanes(b):
    return pl.ds(pl.multiple_of(b * BLK, BLK), BLK)


def compact_rows(code, rank):
    inner_block = (code >> 7) & 7
    border = code - SLOTS
    outer_block = border >> 4
    inner_rank = jnp.full_like(code, NB)
    outer_rank = jnp.full_like(code, NB)
    for b in range(NB):
        inner_rank = jnp.where(inner_block == b, rank[b], inner_rank)
    for k in range(4 * NB):
        outer_rank = jnp.where(outer_block == k, rank[NB + k], outer_rank)
    inner = (code >> 10) * (NF * BLK) + inner_rank * BLK + (code & 127)
    outer = FSLOTS + (border >> 7) * (NF * BFB) + outer_rank * BFB + (border & 15)
    inner = jnp.where(inner_rank < NF, inner, ZROW)
    outer = jnp.where(outer_rank < NF, outer, ZROW)
    return jnp.where(code < SLOTS, inner, outer)


def first_kernel(slots, fields, front, out0, out1, out2, out3, padded, table):
    pad_nodes(fields, padded)
    for b in range(NB):
        lanes = pl.ds(b * BLK, BLK)
        products = node_products(front[0:64], [padded[c, :, lanes] for c in range(6)])
        store_traces(products, table, NB * BLK, b * BLK)
    send_rows(slots, table, [out0, out1, out2, out3], NB * BFB)


def full_kernel(
    codes, send, meta, rank, code_rows, fields, metric, normals, scale, medium, front, lift,
    in0, in1, in2, in3,
    rate, start, rows, out0, out1, out2, out3, padded, table, outer, curl, fine_table,
):
    for f in range(4):
        for i in range(NF):
            rows[f * NF + i : f * NF + i + 1, :] = code_rows[pl.ds(f * NB + meta[i], 1), :]
    rows[...] = compact_rows(rows[...], rank)
    pad_nodes(fields, padded)
    for d, got in enumerate((in0, in1, in2, in3)):
        table[SLOTS + d * NB * BFB : SLOTS + (d + 1) * NB * BFB, :] = got[...]
    for b in range(NB):
        lanes = pl.ds(b * BLK, BLK)
        products = node_products(front[...], [padded[c, :, lanes] for c in range(6)])
        store_traces(products, table, NB * BLK, b * BLK)
        for c, value in enumerate(curls(products, metric, lanes)):
            curl[b, c] = value
    copy_rows(codes, table, outer, SLOTS, 128)
    for b in range(NB):
        lanes = pl.ds(b * BLK, BLK)
        lifted = lifted_flux(outer, table, NB * BLK, b * BLK, normals, scale, lanes, lift[...])
        value = tendency([curl[b, c] for c in range(6)], lifted, medium, lanes)
        for c in range(6):
            curl[b, c] = value[c]
            rate[c, :, lanes] = value[c][:NP]
    for i in range(NF):
        keep = i < meta[NF]
        value = [jnp.where(keep, curl[meta[i], c], 0.0) for c in range(6)]
        for c in range(6):
            start[i, c] = value[c]
        store_traces(node_products(front[0:64], value), fine_table, NF * BLK, i * BLK)
    send_rows(send, fine_table, [out0, out1, out2, out3], NF * BFB)


def fine_update(
    codes, meta, state, start, metric, normals, scale, medium, front, lift, ins, table, outer, curl, emit
):
    for d, got in enumerate(ins):
        at = FSLOTS + d * NF * BFB
        table[at : at + NF * BFB, :] = got[...]
    table[ZROW : ZROW + 8, :] = jnp.zeros((8, BLK), F32)
    for i in range(NF):
        products = node_products(front[...], [state[i, c] for c in range(6)])
        store_traces(products, table, NF * BLK, i * BLK)
        for c, value in enumerate(curls(products, metric, block_lanes(meta[i]))):
            curl[i, c] = value
    copy_rows(codes, table, outer, FSLOTS, 128)
    for i in range(NF):
        lanes = block_lanes(meta[i])
        lifted = lifted_flux(outer, table, NF * BLK, i * BLK, normals, scale, lanes, lift[...])
        value = tendency([curl[i, c] for c in range(6)], lifted, medium, lanes)
        keep = i < meta[NF]
        emit(i, [
            jnp.where(keep, state[i, c] + start[i, c] + STEP * value[c], 0.0) for c in range(6)
        ])


def fine_kernel(
    codes, send, meta, state, start, metric, normals, scale, medium, front, lift, in0, in1, in2, in3,
    new_state, out0, out1, out2, out3, table, outer, curl,
):
    def emit(i, value):
        for c in range(6):
            new_state[i, c] = value[c]

    fine_update(
        codes, meta, state, start, metric, normals, scale, medium, front, lift,
        (in0, in1, in2, in3), table, outer, curl, emit,
    )
    for i in range(NF):
        products = node_products(front[0:64], [new_state[i, c] for c in range(6)])
        store_traces(products, table, NF * BLK, i * BLK)
    send_rows(send, table, [out0, out1, out2, out3], NF * BFB)


def last_kernel(
    codes, meta, state, start, metric, normals, scale, medium, front, lift, in0, in1, in2, in3, rate_in,
    rate, table, outer, curl, result, sem,
):
    def emit(i, value):
        for c in range(6):
            result[i, c] = value[c][:NP] * 0.25

    fine_update(
        codes, meta, state, start, metric, normals, scale, medium, front, lift,
        (in0, in1, in2, in3), table, outer, curl, emit,
    )

    def copy(i):
        return pltpu.make_async_copy(result.at[i], rate.at[:, :, block_lanes(meta[i])], sem.at[i])

    for i in range(NF):
        @pl.when(i < meta[NF])
        def _():
            copy(i).start()

    for i in range(NF):
        @pl.when(i < meta[NF])
        def _():
            copy(i).wait()


def border_slots(codes):
    per_block = codes.reshape(4, NB, BLK).transpose(1, 0, 2).reshape(NB, 1, 4 * BLK)
    side = lax.broadcasted_iota(jnp.int32, (NB, 4 * BFB, 1), 1)
    block = lax.broadcasted_iota(jnp.int32, (NB, 4 * BFB, 1), 0)
    wanted = SLOTS + (side // BFB) * (NB * BFB) + block * BFB + side % BFB
    place = lax.broadcasted_iota(jnp.int32, (NB, 1, 4 * BLK), 2)
    slot = (place // BLK) * (NB * BLK) + lax.broadcasted_iota(jnp.int32, (NB, 1, 4 * BLK), 0) * BLK + place % BLK
    found = jnp.sum(jnp.where(per_block == wanted, slot, 0), axis=2)
    return found.reshape(NB, 4, BFB).transpose(1, 0, 2)


def fine_plan(slots, levels):
    padded = jnp.pad(levels, ((1, 1), (1, 1), (0, 0)))
    near = lax.dynamic_slice(padded, (lax.axis_index("px"), lax.axis_index("py"), 0), (3, 3, NB))
    fine = (jnp.stack([near[1, 1], near[0, 1], near[2, 1], near[1, 0], near[1, 2]]) > 0).astype(jnp.int32)
    before = (jnp.arange(NB)[None, :] < jnp.arange(NB)[:, None]).astype(jnp.int32)
    fine_before = jnp.sum(fine[:, None, :] * before[None], axis=2)
    coarse_before = jnp.sum((1 - fine[:, None, :]) * before[None], axis=2)
    count = jnp.sum(fine, axis=1, keepdims=True)
    rank = jnp.where(fine > 0, fine_before, count + coarse_before)
    ids = jnp.arange(NB, dtype=jnp.int32)
    chosen = rank[0][None, :] == jnp.arange(NF)[:, None]
    order = jnp.sum(jnp.where(chosen, ids[None, :], 0), axis=1)
    meta = jnp.concatenate([order, count[0], jnp.zeros((3,), jnp.int32)])
    slot = jnp.sum(jnp.where(chosen[None, :, :, None], slots[:, None], 0), axis=2)
    send = (slot >> 10) * (NF * BLK) + jnp.arange(NF, dtype=jnp.int32)[None, :, None] * BLK + (slot & 127)
    return meta, rank.reshape(5 * NB), send.reshape(FRECV)


def stacked(matrix):
    hi = lax.reduce_precision(matrix, 8, 7)
    return jnp.concatenate([hi, hi, matrix - hi], axis=1).astype(BF16)


VMEM = pl.BlockSpec(memory_space=pltpu.VMEM)
SMEM = pl.BlockSpec(memory_space=pltpu.SMEM)
ANY = pl.BlockSpec(memory_space=pl.ANY)
PARAMS = pltpu.CompilerParams(vmem_limit_bytes=VMEM_LIMIT)


def cost(flops, size):
    return pl.CostEstimate(flops=flops, bytes_accessed=size, transcendentals=0)


def shards(
    fields, metric, normals, face_scale, permittivity, derivative, face_interp, lift, neighbor, levels
):
    codes = neighbor.reshape(4 * NB, BLK)
    medium = permittivity.reshape(1, NB * BLK)
    slots = border_slots(codes)
    front = jnp.concatenate([
        jnp.pad(face_interp, ((0, 0), (0, 1), (0, KPAD - NP))).reshape(4 * FPAD, KPAD),
        jnp.pad(derivative, ((0, 0), (0, NPAD - NP), (0, KPAD - NP))).reshape(3 * NPAD, KPAD),
        jnp.zeros((8, KPAD), F32),
    ])
    front = stacked(front)
    lift_wide = jnp.pad(lift.reshape(NP, 4, 15), ((0, KPAD - NP), (0, 0), (0, 1)))
    lift_wide = stacked(lift_wide.reshape(KPAD, 4 * FPAD))
    meta, rank, send = fine_plan(slots, levels)

    def exchange(out):
        def ways(axis):
            count = lax.axis_size(axis)
            return [(i, i + 1) for i in range(count - 1)], [(i + 1, i) for i in range(count - 1)]

        x_up, x_down = ways("px")
        y_up, y_down = ways("py")
        return (
            lax.ppermute(out[1], "px", x_up),
            lax.ppermute(out[0], "px", x_down),
            lax.ppermute(out[3], "py", y_up),
            lax.ppermute(out[2], "py", y_down),
        )

    def message(rows_of):
        return [jax.ShapeDtypeStruct((rows_of, BLK), F32)] * 4

    state_shape = jax.ShapeDtypeStruct((NF, 6, NPAD, BLK), F32)
    geometry = (metric, normals, face_scale, medium, front, lift_wide)
    out = pl.pallas_call(
        first_kernel,
        out_shape=message(NB * BFB),
        in_specs=[SMEM, VMEM, VMEM],
        out_specs=[VMEM] * 4,
        scratch_shapes=[pltpu.VMEM((6, NPAD, NB * BLK), F32), pltpu.VMEM((SLOTS, BLK), F32)],
        compiler_params=PARAMS,
        cost_estimate=cost(10**9, 2 * 10**6),
        name="border",
    )(slots.reshape(4 * NB * BFB), fields, front)
    received = exchange(out)
    rate, start, rows, *out = pl.pallas_call(
        full_kernel,
        out_shape=[
            jax.ShapeDtypeStruct((6, NP, NB * BLK), F32),
            state_shape,
            jax.ShapeDtypeStruct((4 * NF, BLK), jnp.int32),
        ] + message(NF * BFB),
        in_specs=[SMEM] * 4 + [VMEM] * 12,
        out_specs=[VMEM] * 7,
        scratch_shapes=[
            pltpu.VMEM((6, NPAD, NB * BLK), F32),
            pltpu.VMEM((TAB, BLK), F32),
            pltpu.VMEM((SLOTS, BLK), F32),
            pltpu.VMEM((NB, 6, NPAD, BLK), F32),
            pltpu.VMEM((FSLOTS, BLK), F32),
        ],
        compiler_params=PARAMS,
        cost_estimate=cost(10**9, 4 * 10**6),
        name="full",
    )(neighbor.reshape(SLOTS), send, meta, rank, codes, fields, *geometry, *received)
    rows = rows.reshape(FSLOTS)
    work = [
        pltpu.VMEM((FTAB, BLK), F32),
        pltpu.VMEM((FSLOTS, BLK), F32),
        pltpu.VMEM((NF, 6, NPAD, BLK), F32),
    ]
    state = start
    for _ in range(2):
        received = exchange(out)
        state, *out = pl.pallas_call(
            fine_kernel,
            out_shape=[state_shape] + message(NF * BFB),
            in_specs=[SMEM] * 3 + [VMEM] * 12,
            out_specs=[VMEM] * 5,
            scratch_shapes=work,
            compiler_params=PARAMS,
            cost_estimate=cost(10**9, 2 * 10**6),
            name="fine",
        )(rows, send, meta, state, start, *geometry, *received)
    received = exchange(out)
    return pl.pallas_call(
        last_kernel,
        out_shape=jax.ShapeDtypeStruct((6, NP, NB * BLK), F32),
        in_specs=[SMEM] * 2 + [VMEM] * 12 + [ANY],
        out_specs=ANY,
        scratch_shapes=work + [pltpu.VMEM((NF, 6, NP, BLK), F32), pltpu.SemaphoreType.DMA((NF,))],
        input_output_aliases={14: 0},
        compiler_params=PARAMS,
        cost_estimate=cost(10**9, 2 * 10**6),
        name="last",
    )(rows, meta, state, start, *geometry, *received, rate)


def solution(mesh):
    in_specs = (
        P(None, None, ("px", "py")),
        P(None, None, ("px", "py")),
        P(None, None, ("px", "py")),
        P(None, ("px", "py")),
        P(("px", "py")),
        P(),
        P(),
        P(),
        P("px", "py", None),
        P(),
    )
    out_specs = P(None, None, ("px", "py"))
    return jax.shard_map(shards, mesh=mesh, in_specs=in_specs, out_specs=out_specs, check_vma=False)
```

profile of v0, /device:TPU:6, one launch (start us, length us, event | category | flops | bytes accessed | tf_op | source)
XLA Modules:
  0.0 102.0 jit_solution(17872372380396099894)
XLA Ops:
  4.4 2.0 %border.1 = (f32[128,128]{1,0:T(8,128)S(1)}, f32[128,128]{1,0:T(8,128)S(1)}, f32[128,128]{1,0:T(8,128)S(1)}, f32[128,128]{1,0:T(8,128)S(1)}) custom-call(s32[512]{0:T(512)S(1)} %reshape.351.slots, f32[6,35,1024]{2,1,0:T(8,128)S(1)} %copy-done.1, bf16[192,144]{1,0:T(8,128)(2,1)S(1)} %pad_maximum_fusion.front), custom_call_target="tpu_custom_call" | custom-call | flops 1000000000 | bytes 2000000 | tf_op jit(solution)/shard_map/border/pallas_call | solution.py:334
  6.4 2.1 %collective-permute-start = (f32[128,128]{1,0:T(8,128)S(1)}, f32[128,128]{1,0:T(8,128)S(1)}, u32[]{:S(2)}, u32[]{:S(2)}) collective-permute-start(f32[128,128]{1,0:T(8,128)S(1)} %get-tuple-element.26), channel_id=1, source_target_pairs={{0,12},{12,24},{24,36},{36,48},{48,60},{60,72},{72,84},{84,96},{96... | collective-permute-start | bytes 196616 | tf_op jit(solution)/shard_map/ppermute | solution.py:323
  8.5 5.8 %collective-permute-start.1 = (f32[128,128]{1,0:T(8,128)S(1)}, f32[128,128]{1,0:T(8,128)S(1)}, u32[]{:S(2)}, u32[]{:S(2)}) collective-permute-start(f32[128,128]{1,0:T(8,128)S(1)} %get-tuple-element.27), channel_id=1, source_target_pairs={{12,0},{24,12},{36,24},{48,36},{60,48},{72,60},{84,72},{96,84},{10... | collective-permute-start | bytes 196616 | tf_op jit(solution)/shard_map/ppermute | solution.py:324
  14.2 4.3 %collective-permute-start.2 = (f32[128,128]{1,0:T(8,128)S(1)}, f32[128,128]{1,0:T(8,128)S(1)}, u32[]{:S(2)}, u32[]{:S(2)}) collective-permute-start(f32[128,128]{1,0:T(8,128)S(1)} %get-tuple-element.28), channel_id=1, source_target_pairs={{0,1},{1,2},{2,3},{3,4},{4,5},{5,6},{6,7},{7,8},{8,9},{9,10},{10,1... | collective-permute-start | bytes 196616 | tf_op jit(solution)/shard_map/ppermute | solution.py:325
  18.5 1.3 %collective-permute-start.3 = (f32[128,128]{1,0:T(8,128)S(1)}, f32[128,128]{1,0:T(8,128)S(1)}, u32[]{:S(2)}, u32[]{:S(2)}) collective-permute-start(f32[128,128]{1,0:T(8,128)S(1)} %get-tuple-element.29), channel_id=1, source_target_pairs={{1,0},{2,1},{3,2},{4,3},{5,4},{6,5},{7,6},{8,7},{9,8},{10,9},{11,1... | collective-permute-start | bytes 196616 | tf_op jit(solution)/shard_map/ppermute | solution.py:326
  22.0 3.0 %collective-permute-done.3.in3 = f32[128,128]{1,0:T(8,128)S(1)} collective-permute-done((f32[128,128]{1,0:T(8,128)S(1)}, f32[128,128]{1,0:T(8,128)S(1)}, u32[]{:S(2)}, u32[]{:S(2)}) %collective-permute-start.3) | collective-permute-done | bytes 65568 | tf_op jit(solution)/shard_map/ppermute | solution.py:326
  25.1 8.1 %full.1 = (f32[6,35,1024]{2,1,0:T(8,128)}, f32[4,6,40,128]{3,2,1,0:T(8,128)S(1)}, s32[16,128]{1,0:T(8,128)S(1)}, f32[64,128]{1,0:T(8,128)S(1)}, f32[64,128]{1,0:...) custom-call(s32[4096]{0:T(1024)S(1)} %bitcast.24, s32[256]{0:T(256)S(1)} %add.117.send, ...), custom_call_target="tpu_custom_call" | custom-call | flops 1000000000 | bytes 4000000 | tf_op jit(solution)/shard_map/full/pallas_call | solution.py:345
  33.1 1.9 %collective-permute-start.4 = (f32[64,128]{1,0:T(8,128)S(1)}, f32[64,128]{1,0:T(8,128)S(1)}, u32[]{:S(2)}, u32[]{:S(2)}) collective-permute-start(f32[64,128]{1,0:T(8,128)S(1)} %get-tuple-element.32), channel_id=1, source_target_pairs={{0,12},{12,24},{24,36},{36,48},{48,60},{60,72},{72,84},{84,96},{96... | collective-permute-start | bytes 98312 | tf_op jit(solution)/shard_map/ppermute | solution.py:323
  35.0 5.8 %collective-permute-start.5 = (f32[64,128]{1,0:T(8,128)S(1)}, f32[64,128]{1,0:T(8,128)S(1)}, u32[]{:S(2)}, u32[]{:S(2)}) collective-permute-start(f32[64,128]{1,0:T(8,128)S(1)} %get-tuple-element.33), channel_id=1, source_target_pairs={{12,0},{24,12},{36,24},{48,36},{60,48},{72,60},{84,72},{96,84},{10... | collective-permute-start | bytes 98312 | tf_op jit(solution)/shard_map/ppermute | solution.py:324
  40.8 4.3 %collective-permute-start.6 = (f32[64,128]{1,0:T(8,128)S(1)}, f32[64,128]{1,0:T(8,128)S(1)}, u32[]{:S(2)}, u32[]{:S(2)}) collective-permute-start(f32[64,128]{1,0:T(8,128)S(1)} %get-tuple-element.34), channel_id=1, source_target_pairs={{0,1},{1,2},{2,3},{3,4},{4,5},{5,6},{6,7},{7,8},{8,9},{9,10},{10,1... | collective-permute-start | bytes 98312 | tf_op jit(solution)/shard_map/ppermute | solution.py:325
  45.1 1.3 %collective-permute-start.7 = (f32[64,128]{1,0:T(8,128)S(1)}, f32[64,128]{1,0:T(8,128)S(1)}, u32[]{:S(2)}, u32[]{:S(2)}) collective-permute-start(f32[64,128]{1,0:T(8,128)S(1)} %get-tuple-element.35), channel_id=1, source_target_pairs={{1,0},{2,1},{3,2},{4,3},{5,4},{6,5},{7,6},{8,7},{9,8},{10,9},{11,1... | collective-permute-start | bytes 98312 | tf_op jit(solution)/shard_map/ppermute | solution.py:326
  46.7 5.8 %collective-permute-done.7.in3 = f32[64,128]{1,0:T(8,128)S(1)} collective-permute-done((f32[64,128]{1,0:T(8,128)S(1)}, f32[64,128]{1,0:T(8,128)S(1)}, u32[]{:S(2)}, u32[]{:S(2)}) %collective-permute-start.7) | collective-permute-done | bytes 32800 | tf_op jit(solution)/shard_map/ppermute | solution.py:326
  52.5 4.2 %fine.2 = (f32[4,6,40,128]{3,2,1,0:T(8,128)S(1)}, f32[64,128]{1,0:T(8,128)S(1)}, f32[64,128]{1,0:T(8,128)S(1)}, f32[64,128]{1,0:T(8,128)S(1)}, f32[64,128]{1,0:T(8,128)S(1)}) custom-call(s32[2048]{0:T(1024)S(1)} %bitcast.30, s32[256]{0:T(256)S(1)} %add.117.send, s32[8]{0:T(128)S(1)} %pad_add_fusion.meta, ...), custom_call_target="tpu_custom_call" | custom-call | flops 1000000000 | bytes 2000000 | tf_op jit(solution)/shard_map/fine/pallas_call | solution.py:374
  56.7 1.9 %collective-permute-start.8 = (f32[64,128]{1,0:T(8,128)S(1)}, f32[64,128]{1,0:T(8,128)S(1)}, u32[]{:S(2)}, u32[]{:S(2)}) collective-permute-start(f32[64,128]{1,0:T(8,128)S(1)} %get-tuple-element.37), channel_id=1, source_target_pairs={{0,12},{12,24},{24,36},{36,48},{48,60},{60,72},{72,84},{84,96},{96... | collective-permute-start | bytes 98312 | tf_op jit(solution)/shard_map/ppermute | solution.py:323
  58.6 5.8 %collective-permute-start.9 = (f32[64,128]{1,0:T(8,128)S(1)}, f32[64,128]{1,0:T(8,128)S(1)}, u32[]{:S(2)}, u32[]{:S(2)}) collective-permute-start(f32[64,128]{1,0:T(8,128)S(1)} %get-tuple-element.38), channel_id=1, source_target_pairs={{12,0},{24,12},{36,24},{48,36},{60,48},{72,60},{84,72},{96,84},{10... | collective-permute-start | bytes 98312 | tf_op jit(solution)/shard_map/ppermute | solution.py:324
  64.4 5.1 %collective-permute-start.10 = (f32[64,128]{1,0:T(8,128)S(1)}, f32[64,128]{1,0:T(8,128)S(1)}, u32[]{:S(2)}, u32[]{:S(2)}) collective-permute-start(f32[64,128]{1,0:T(8,128)S(1)} %get-tuple-element.39), channel_id=1, source_target_pairs={{0,1},{1,2},{2,3},{3,4},{4,5},{5,6},{6,7},{7,8},{8,9},{9,10},{10,1... | collective-permute-start | bytes 98312 | tf_op jit(solution)/shard_map/ppermute | solution.py:325
  69.5 1.3 %collective-permute-start.11 = (f32[64,128]{1,0:T(8,128)S(1)}, f32[64,128]{1,0:T(8,128)S(1)}, u32[]{:S(2)}, u32[]{:S(2)}) collective-permute-start(f32[64,128]{1,0:T(8,128)S(1)} %get-tuple-element.40), channel_id=1, source_target_pairs={{1,0},{2,1},{3,2},{4,3},{5,4},{6,5},{7,6},{8,7},{9,8},{10,9},{11,1... | collective-permute-start | bytes 98312 | tf_op jit(solution)/shard_map/ppermute | solution.py:326
  71.1 4.2 %collective-permute-done.11.in3 = f32[64,128]{1,0:T(8,128)S(1)} collective-permute-done((f32[64,128]{1,0:T(8,128)S(1)}, f32[64,128]{1,0:T(8,128)S(1)}, u32[]{:S(2)}, u32[]{:S(2)}) %collective-permute-start.11) | collective-permute-done | bytes 32800 | tf_op jit(solution)/shard_map/ppermute | solution.py:326
  75.3 4.2 %fine.3 = (f32[4,6,40,128]{3,2,1,0:T(8,128)S(1)}, f32[64,128]{1,0:T(8,128)S(1)}, f32[64,128]{1,0:T(8,128)S(1)}, f32[64,128]{1,0:T(8,128)S(1)}, f32[64,128]{1,0:T(8,128)S(1)}) custom-call(s32[2048]{0:T(1024)S(1)} %bitcast.31, s32[256]{0:T(256)S(1)} %add.117.send, s32[8]{0:T(128)S(1)} %pad_add_fusion.meta, f32[4,6,40,128]{3,2,1,0:T(8,128)S(1)} %get-tuple-element.36.state, ...), custom_call_target="tpu_custom_call" | custom-call | flops 1000000000 | bytes 2000000 | tf_op jit(solution)/shard_map/fine/pallas_call | solution.py:374
  79.6 1.9 %collective-permute-start.12 = (f32[64,128]{1,0:T(8,128)S(1)}, f32[64,128]{1,0:T(8,128)S(1)}, u32[]{:S(2)}, u32[]{:S(2)}) collective-permute-start(f32[64,128]{1,0:T(8,128)S(1)} %get-tuple-element.42), channel_id=1, source_target_pairs={{0,12},{12,24},{24,36},{36,48},{48,60},{60,72},{72,84},{84,96},{96... | collective-permute-start | bytes 98312 | tf_op jit(solution)/shard_map/ppermute | solution.py:323
  81.5 5.8 %collective-permute-start.13 = (f32[64,128]{1,0:T(8,128)S(1)}, f32[64,128]{1,0:T(8,128)S(1)}, u32[]{:S(2)}, u32[]{:S(2)}) collective-permute-start(f32[64,128]{1,0:T(8,128)S(1)} %get-tuple-element.43), channel_id=1, source_target_pairs={{12,0},{24,12},{36,24},{48,36},{60,48},{72,60},{84,72},{96,84},{10... | collective-permute-start | bytes 98312 | tf_op jit(solution)/shard_map/ppermute | solution.py:324
  87.3 4.6 %collective-permute-start.14 = (f32[64,128]{1,0:T(8,128)S(1)}, f32[64,128]{1,0:T(8,128)S(1)}, u32[]{:S(2)}, u32[]{:S(2)}) collective-permute-start(f32[64,128]{1,0:T(8,128)S(1)} %get-tuple-element.44), channel_id=1, source_target_pairs={{0,1},{1,2},{2,3},{3,4},{4,5},{5,6},{6,7},{7,8},{8,9},{9,10},{10,1... | collective-permute-start | bytes 98312 | tf_op jit(solution)/shard_map/ppermute | solution.py:325
  93.5 4.2 %collective-permute-done.15.in3 = f32[64,128]{1,0:T(8,128)S(1)} collective-permute-done((f32[64,128]{1,0:T(8,128)S(1)}, f32[64,128]{1,0:T(8,128)S(1)}, u32[]{:S(2)}, u32[]{:S(2)}) %collective-permute-start.15) | collective-permute-done | bytes 32800 | tf_op jit(solution)/shard_map/ppermute | solution.py:326
  97.7 4.2 %last.1 = f32[6,35,1024]{2,1,0:T(8,128)} custom-call(s32[2048]{0:T(1024)S(1)} %bitcast.32, s32[8]{0:T(128)S(1)} %pad_add_fusion.meta, f32[4,6,40,128]{3,2,1,0:T(8,128)S(1)} %get-tuple-element.41.state, f32[4,6,40,128]{3,2,1,0:T(8,128)S(1)} %get-tuple-element.31.state.start, f32[3,3,1024]{2,1,0:T(4,128)S(1)} %copy-done.3, ...), custom_call_target="tpu_custom_call", output_to_operand_aliasing={{}: (14, {})} | custom-call | flops 1000000000 | bytes 2000000 | tf_op jit(solution)/shard_map/last/pallas_call | solution.py:385
  (80 shorter events, 8.5 us)
Async XLA Ops:
  2.0 0.8 copy-start.7
  3.2 1.2 %copy-start.1 = (f32[6,35,1024]{2,1,0:T(8,128)S(1)}, f32[6,35,1024]{2,1,0:T(8,128)}, u32[]{:S(2)}) copy-start(f32[6,35,1024]{2,1,0:T(8,128)} %fields.3) | copy-start | bytes 2580484
  4.4 20.6 %copy-start.2 = (f32[6,35,1024]{2,1,0:T(8,128)S(1)}, f32[6,35,1024]{2,1,0:T(8,128)}, u32[]{:S(2)}) copy-start(f32[6,35,1024]{2,1,0:T(8,128)} %fields.3) | copy-start | bytes 2580484
  6.4 13.5 %copy-start.8 = (s32[64,12,8]{0,2,1:T(8,128)S(1)}, s32[64,12,8]{0,2,1:T(8,128)}, u32[]{:S(2)}) copy-start(s32[64,12,8]{0,2,1:T(8,128)} %param.19) | copy-start | bytes 73732
  6.4 15.6 %collective-permute-start = (f32[128,128]{1,0:T(8,128)S(1)}, f32[128,128]{1,0:T(8,128)S(1)}, u32[]{:S(2)}, u32[]{:S(2)}) collective-permute-start(f32[128,128]{1,0:T(8,128)S(1)} %get-tuple-element.26), channel_id=1, source_target_pairs={{0,12},{12,24},{24,36},{36,48},{48,60},{60,72},{72,84},{84,96},{96... | collective-permute-start | bytes 196616 | tf_op jit(solution)/shard_map/ppermute | solution.py:323
  8.5 13.5 %collective-permute-start.1 = (f32[128,128]{1,0:T(8,128)S(1)}, f32[128,128]{1,0:T(8,128)S(1)}, u32[]{:S(2)}, u32[]{:S(2)}) collective-permute-start(f32[128,128]{1,0:T(8,128)S(1)} %get-tuple-element.27), channel_id=1, source_target_pairs={{12,0},{24,12},{36,24},{48,36},{60,48},{72,60},{84,72},{96,84},{10... | collective-permute-start | bytes 196616 | tf_op jit(solution)/shard_map/ppermute | solution.py:324
  14.2 7.8 %collective-permute-start.2 = (f32[128,128]{1,0:T(8,128)S(1)}, f32[128,128]{1,0:T(8,128)S(1)}, u32[]{:S(2)}, u32[]{:S(2)}) collective-permute-start(f32[128,128]{1,0:T(8,128)S(1)} %get-tuple-element.28), channel_id=1, source_target_pairs={{0,1},{1,2},{2,3},{3,4},{4,5},{5,6},{6,7},{7,8},{8,9},{9,10},{10,1... | collective-permute-start | bytes 196616 | tf_op jit(solution)/shard_map/ppermute | solution.py:325
  18.5 6.5 %collective-permute-start.3 = (f32[128,128]{1,0:T(8,128)S(1)}, f32[128,128]{1,0:T(8,128)S(1)}, u32[]{:S(2)}, u32[]{:S(2)}) collective-permute-start(f32[128,128]{1,0:T(8,128)S(1)} %get-tuple-element.29), channel_id=1, source_target_pairs={{1,0},{2,1},{3,2},{4,3},{5,4},{6,5},{7,6},{8,7},{9,8},{10,9},{11,1... | collective-permute-start | bytes 196616 | tf_op jit(solution)/shard_map/ppermute | solution.py:326
  21.7 3.3 %copy-start.5 = (f32[4,1024]{1,0:T(4,128)S(1)}, f32[4,1024]{1,0:T(4,128)}, u32[]{:S(2)}) copy-start(f32[4,1024]{1,0:T(4,128)} %scale.7) | copy-start | bytes 49156
  21.8 3.3 %copy-start.3 = (f32[3,3,1024]{2,1,0:T(4,128)S(1)}, f32[3,3,1024]{2,1,0:T(4,128)}, u32[]{:S(2)}) copy-start(f32[3,3,1024]{2,1,0:T(4,128)} %metric.7) | copy-start | bytes 110596
  21.8 3.3 %copy-start.4 = (f32[3,4,1024]{2,1,0:T(4,128)S(1)}, f32[3,4,1024]{2,1,0:T(4,128)}, u32[]{:S(2)}) copy-start(f32[3,4,1024]{2,1,0:T(4,128)} %normals.7) | copy-start | bytes 147460
  21.9 3.2 %copy-start.6 = (f32[1024]{0:T(1024)S(1)}, f32[1024]{0:T(1024)}, u32[]{:S(2)}) copy-start(f32[1024]{0:T(1024)} %param.14) | copy-start | bytes 12292
  33.1 13.3 %collective-permute-start.4 = (f32[64,128]{1,0:T(8,128)S(1)}, f32[64,128]{1,0:T(8,128)S(1)}, u32[]{:S(2)}, u32[]{:S(2)}) collective-permute-start(f32[64,128]{1,0:T(8,128)S(1)} %get-tuple-element.32), channel_id=1, source_target_pairs={{0,12},{12,24},{24,36},{36,48},{48,60},{60,72},{72,84},{84,96},{96... | collective-permute-start | bytes 98312 | tf_op jit(solution)/shard_map/ppermute | solution.py:323
  35.0 11.4 %collective-permute-start.5 = (f32[64,128]{1,0:T(8,128)S(1)}, f32[64,128]{1,0:T(8,128)S(1)}, u32[]{:S(2)}, u32[]{:S(2)}) collective-permute-start(f32[64,128]{1,0:T(8,128)S(1)} %get-tuple-element.33), channel_id=1, source_target_pairs={{12,0},{24,12},{36,24},{48,36},{60,48},{72,60},{84,72},{96,84},{10... | collective-permute-start | bytes 98312 | tf_op jit(solution)/shard_map/ppermute | solution.py:324
  40.8 5.9 %collective-permute-start.6 = (f32[64,128]{1,0:T(8,128)S(1)}, f32[64,128]{1,0:T(8,128)S(1)}, u32[]{:S(2)}, u32[]{:S(2)}) collective-permute-start(f32[64,128]{1,0:T(8,128)S(1)} %get-tuple-element.34), channel_id=1, source_target_pairs={{0,1},{1,2},{2,3},{3,4},{4,5},{5,6},{6,7},{7,8},{8,9},{9,10},{10,1... | collective-permute-start | bytes 98312 | tf_op jit(solution)/shard_map/ppermute | solution.py:325
  45.1 7.4 %collective-permute-start.7 = (f32[64,128]{1,0:T(8,128)S(1)}, f32[64,128]{1,0:T(8,128)S(1)}, u32[]{:S(2)}, u32[]{:S(2)}) collective-permute-start(f32[64,128]{1,0:T(8,128)S(1)} %get-tuple-element.35), channel_id=1, source_target_pairs={{1,0},{2,1},{3,2},{4,3},{5,4},{6,5},{7,6},{8,7},{9,8},{10,9},{11,1... | collective-permute-start | bytes 98312 | tf_op jit(solution)/shard_map/ppermute | solution.py:326
  56.7 14.1 %collective-permute-start.8 = (f32[64,128]{1,0:T(8,128)S(1)}, f32[64,128]{1,0:T(8,128)S(1)}, u32[]{:S(2)}, u32[]{:S(2)}) collective-permute-start(f32[64,128]{1,0:T(8,128)S(1)} %get-tuple-element.37), channel_id=1, source_target_pairs={{0,12},{12,24},{24,36},{36,48},{48,60},{60,72},{72,84},{84,96},{96... | collective-permute-start | bytes 98312 | tf_op jit(solution)/shard_map/ppermute | solution.py:323
  58.6 12.2 %collective-permute-start.9 = (f32[64,128]{1,0:T(8,128)S(1)}, f32[64,128]{1,0:T(8,128)S(1)}, u32[]{:S(2)}, u32[]{:S(2)}) collective-permute-start(f32[64,128]{1,0:T(8,128)S(1)} %get-tuple-element.38), channel_id=1, source_target_pairs={{12,0},{24,12},{36,24},{48,36},{60,48},{72,60},{84,72},{96,84},{10... | collective-permute-start | bytes 98312 | tf_op jit(solution)/shard_map/ppermute | solution.py:324
  64.4 6.7 %collective-permute-start.10 = (f32[64,128]{1,0:T(8,128)S(1)}, f32[64,128]{1,0:T(8,128)S(1)}, u32[]{:S(2)}, u32[]{:S(2)}) collective-permute-start(f32[64,128]{1,0:T(8,128)S(1)} %get-tuple-element.39), channel_id=1, source_target_pairs={{0,1},{1,2},{2,3},{3,4},{4,5},{5,6},{6,7},{7,8},{8,9},{9,10},{10,1... | collective-permute-start | bytes 98312 | tf_op jit(solution)/shard_map/ppermute | solution.py:325
  69.5 5.8 %collective-permute-start.11 = (f32[64,128]{1,0:T(8,128)S(1)}, f32[64,128]{1,0:T(8,128)S(1)}, u32[]{:S(2)}, u32[]{:S(2)}) collective-permute-start(f32[64,128]{1,0:T(8,128)S(1)} %get-tuple-element.40), channel_id=1, source_target_pairs={{1,0},{2,1},{3,2},{4,3},{5,4},{6,5},{7,6},{8,7},{9,8},{10,9},{11,1... | collective-permute-start | bytes 98312 | tf_op jit(solution)/shard_map/ppermute | solution.py:326
  79.6 13.6 %collective-permute-start.12 = (f32[64,128]{1,0:T(8,128)S(1)}, f32[64,128]{1,0:T(8,128)S(1)}, u32[]{:S(2)}, u32[]{:S(2)}) collective-permute-start(f32[64,128]{1,0:T(8,128)S(1)} %get-tuple-element.42), channel_id=1, source_target_pairs={{0,12},{12,24},{24,36},{36,48},{48,60},{60,72},{72,84},{84,96},{96... | collective-permute-start | bytes 98312 | tf_op jit(solution)/shard_map/ppermute | solution.py:323
  81.5 11.7 %collective-permute-start.13 = (f32[64,128]{1,0:T(8,128)S(1)}, f32[64,128]{1,0:T(8,128)S(1)}, u32[]{:S(2)}, u32[]{:S(2)}) collective-permute-start(f32[64,128]{1,0:T(8,128)S(1)} %get-tuple-element.43), channel_id=1, source_target_pairs={{12,0},{24,12},{36,24},{48,36},{60,48},{72,60},{84,72},{96,84},{10... | collective-permute-start | bytes 98312 | tf_op jit(solution)/shard_map/ppermute | solution.py:324
  87.3 6.2 %collective-permute-start.14 = (f32[64,128]{1,0:T(8,128)S(1)}, f32[64,128]{1,0:T(8,128)S(1)}, u32[]{:S(2)}, u32[]{:S(2)}) collective-permute-start(f32[64,128]{1,0:T(8,128)S(1)} %get-tuple-element.44), channel_id=1, source_target_pairs={{0,1},{1,2},{2,3},{3,4},{4,5},{5,6},{6,7},{7,8},{8,9},{9,10},{10,1... | collective-permute-start | bytes 98312 | tf_op jit(solution)/shard_map/ppermute | solution.py:325
  91.9 5.8 %collective-permute-start.15 = (f32[64,128]{1,0:T(8,128)S(1)}, f32[64,128]{1,0:T(8,128)S(1)}, u32[]{:S(2)}, u32[]{:S(2)}) collective-permute-start(f32[64,128]{1,0:T(8,128)S(1)} %get-tuple-element.45), channel_id=1, source_target_pairs={{1,0},{2,1},{3,2},{4,3},{5,4},{6,5},{7,6},{8,7},{9,8},{10,9},{11,1... | collective-permute-start | bytes 98312 | tf_op jit(solution)/shard_map/ppermute | solution.py:326
  (3 other events, 2.2 us)
where the time goes:
time: 103 us; the launch traced here: 102 us
  starting transfers between devices  54.3 us (53%)
  Pallas kernels  22.7 us (22%)
  waiting for transfers between devices  18.1 us (18%)
  local copies, waits for them, and re-layouts  4.73 us (5%)
  other arithmetic  1.69 us (2%)
    ppermute x4, starting transfers between devices, exchange(): lax.ppermute(out[0], 'px', x_down)  23 us
    ppermute x4, starting transfers between devices, exchange(): lax.ppermute(out[3], 'py', y_up)  18.3 us
    ppermute x4, waiting for transfers between devices, exchange(): lax.ppermute(out[2], 'py', y_down)  17.3 us
    pallas_call x2, Pallas kernels, shards(): pl.pallas_call(fine_kernel, out_shape=[state_shape] + message(NF * BFB),...  8.48 us
    pallas_call x1, Pallas kernels, shards(): pl.pallas_call(full_kernel, out_shape=[jax.ShapeDtypeStruct((6, NP, NB *...  8.06 us
    ppermute x4, starting transfers between devices, exchange(): lax.ppermute(out[1], 'px', x_up)  7.8 us
    ppermute x4, starting transfers between devices, exchange(): lax.ppermute(out[2], 'py', y_down)  5.17 us
    pallas_call x1, Pallas kernels, shards(): pl.pallas_call(last_kernel, out_shape=jax.ShapeDtypeStruct((6, NP, NB * B...  4.24 us
  transfers between devices with their start and end apart: 16, of which 7 were waited for; matrix products, arithmetic and copies ran while one was open for 2% of the time, Pallas kernels for 0%

commit v1 on v0

v1 whole, which is shorter than its diff:
```python
import jax
import jax.numpy as jnp
from jax import lax
from jax.experimental import pallas as pl
from jax.experimental.pallas import tpu as pltpu
from jax.sharding import PartitionSpec as P

F32 = jnp.float32
BF16 = jnp.bfloat16
BLK = 128
BFB = 16
NB = 8
NF = 4
NP = 35
NPAD = 40
KLIFT = 48
KROWS = 128
FPAD = 16
STEP = 0.05
SLOTS = 4 * NB * BLK
FSLOTS = 4 * NF * BLK
FRECV = 4 * NF * BFB
ZROW = FSLOTS
TAB = SLOTS + 4 * NB * BFB
FTAB = ZROW + 8
TRASH = FSLOTS
VMEM_LIMIT = 16 * 1024 * 1024


def split(x):
    hi = x.astype(BF16)
    lo = (x - hi.astype(F32)).astype(BF16)
    return hi, lo


def node_products(matrix, nodal):
    wide = jnp.concatenate(nodal, axis=1)
    hi = wide.astype(BF16).astype(F32)
    zero = jnp.zeros((KROWS - 3 * NPAD, 6 * BLK), F32)
    wide = jnp.concatenate([hi, wide - hi, hi, zero], axis=0).astype(BF16)
    return jnp.dot(matrix, wide, preferred_element_type=F32)


def stacked(matrix):
    hi = matrix.astype(BF16).astype(F32)
    return (hi + pltpu.roll(hi, NPAD, 1) + pltpu.roll(matrix - hi, 2 * NPAD, 1)).astype(BF16)


def store_traces(products, table, stride, base):
    for f in range(4):
        rows = products[f * FPAD : (f + 1) * FPAD]
        parts = [rows[:, c * BLK : (c + 1) * BLK] for c in range(6)]
        tile = jnp.concatenate(parts + [jnp.zeros((BLK - 6 * FPAD, BLK), F32)], axis=0)
        table[pl.ds(f * stride + base, BLK), :] = tile.T


def curls(products, metric, lanes):
    def nodal(a, c):
        return products[a * NPAD : (a + 1) * NPAD, c * BLK : (c + 1) * BLK]

    rows = [[metric[i, a : a + 1, lanes] for a in range(3)] for i in range(3)]

    def grad(i, c):
        return rows[i][0] * nodal(0, c) + rows[i][1] * nodal(1, c) + rows[i][2] * nodal(2, c)

    curl_h = [grad(1, 5) - grad(2, 4), grad(2, 3) - grad(0, 5), grad(0, 4) - grad(1, 3)]
    curl_e = [grad(1, 2) - grad(2, 1), grad(2, 0) - grad(0, 2), grad(0, 1) - grad(1, 0)]
    return curl_h + curl_e


def cross(n, v):
    return [n[1] * v[2] - n[2] * v[1], n[2] * v[0] - n[0] * v[2], n[0] * v[1] - n[1] * v[0]]


def lifted_flux(outer, table, stride, base, normals, scale, lanes, lift):
    faces = [[], [], [], [], [], []]
    for f in range(4):
        at = pl.ds(f * stride + base, BLK)
        jump = (outer[at, :] - table[at, :]).T
        de = [jump[c * FPAD : (c + 1) * FPAD] for c in range(3)]
        dh = [jump[c * FPAD : (c + 1) * FPAD] for c in range(3, 6)]
        n = [normals[i, f : f + 1, lanes] for i in range(3)]
        half = 0.5 * scale[f : f + 1, lanes]
        dot_e = n[0] * de[0] + n[1] * de[1] + n[2] * de[2]
        dot_h = n[0] * dh[0] + n[1] * dh[1] + n[2] * dh[2]
        nh = cross(n, dh)
        ne = cross(n, de)
        for i in range(3):
            faces[i].append((nh[i] + de[i] - dot_e * n[i]) * half)
            faces[3 + i].append((dh[i] - dot_h * n[i] - ne[i]) * half)
    wide = jnp.concatenate([jnp.concatenate(x, axis=0) for x in faces], axis=1)
    hi, lo = split(wide)
    out = jnp.dot(lift[:, : 12 * FPAD], jnp.concatenate([hi, lo, hi], axis=0), preferred_element_type=F32)
    return [out[:NPAD, c * BLK : (c + 1) * BLK] for c in range(6)]


def tendency(curl, lifted, medium, lanes):
    inverse = 1.0 / medium[:, lanes]
    electric = [(curl[c] + lifted[c]) * inverse for c in range(3)]
    return electric + [lifted[c] - curl[c] for c in range(3, 6)]


def copy_rows(index, source, target, base):
    for r in range(BLK):
        target[pl.ds(base + r, 1), :] = source[pl.ds(index[base + r], 1), :]


def send_rows(index, table, outs):
    for d in range(4):
        for i in range(NF):
            for w in range(BFB):
                r = i * BFB + w
                outs[d][r : r + 1, :] = table[pl.ds(index[i, d * BFB + w], 1), :]


def pad_nodes(fields, padded, lo, hi):
    for c in range(6):
        padded[c, 32:NPAD, lo:hi] = jnp.zeros((NPAD - 32, hi - lo), F32)
        padded[c, 0:NP, lo:hi] = fields[c, :, lo:hi]


def block_lanes(b):
    return pl.ds(b * BLK if isinstance(b, int) else pl.multiple_of(b * BLK, BLK), BLK)


def each(count, body):
    for b in range(count):
        body(b)


def compact_rows(code, rank):
    block = (code >> 7) & 7
    place = jnp.full_like(code, NB)
    for b in range(NB):
        place = jnp.where(block == b, rank[0, b], place)
    row = (code >> 10) * (NF * BLK) + place * BLK + (code & 127)
    return jnp.where((code < SLOTS) & (place < NF), row, ZROW)


def find_slots(codes, wide, index):
    wide[...] = jnp.zeros_like(wide)
    wide[0 : 4 * NB, :] = codes[...].astype(F32)
    columns = wide[...].T
    lane = lax.broadcasted_iota(jnp.int32, (BLK, BLK), 1)
    element = lax.broadcasted_iota(jnp.int32, (BLK, BLK), 0).astype(F32)
    for b in range(NB):
        wanted = (SLOTS + (lane >> 4) * (NB * BFB) + b * BFB + (lane & 15)).astype(F32)
        found = jnp.zeros((BLK, BLK), F32)
        for f in range(4):
            column = columns[:, f * NB + b : f * NB + b + 1]
            found += jnp.where(column == wanted, element + (f * NB + b) * BLK, 0.0)
        index[b : b + 1, :] = jnp.sum(found, axis=0, keepdims=True).astype(jnp.int32)


def first_kernel(
    code_rows, fields, interp, slots, table, front, out0, out1, out2, out3,
    padded, raw, code_buf, interp_buf, wide, index, sem,
):
    half = NB * BLK // 2
    copies = [
        pltpu.make_async_copy(code_rows, code_buf, sem.at[0]),
        pltpu.make_async_copy(interp, interp_buf, sem.at[1]),
    ] + [
        pltpu.make_async_copy(
            fields.at[:, :, h * half : (h + 1) * half], raw.at[:, :, h * half : (h + 1) * half], sem.at[2 + h]
        )
        for h in range(2)
    ]
    for copy in copies:
        copy.start()
    table[SLOTS:TAB, :] = jnp.zeros((TAB - SLOTS, BLK), F32)
    copies[0].wait()
    find_slots(code_buf, wide, slots)
    to_scalar = pltpu.make_async_copy(slots, index, sem.at[4])
    to_scalar.start()
    copies[1].wait()
    wide[...] = jnp.zeros_like(wide)
    for f in range(4):
        for m in range(15):
            wide[f * FPAD + m : f * FPAD + m + 1, 0:NP] = interp_buf[m, f : f + 1, :]
    front[...] = stacked(wide[0 : 4 * FPAD, :])
    for h in range(2):
        copies[2 + h].wait()
        pad_nodes(raw, padded, h * half, (h + 1) * half)

        def traces(i, h=h):
            b = i + h * NB // 2
            lanes = block_lanes(b)
            products = node_products(front[...], [padded[c, :, lanes] for c in range(6)])
            store_traces(products, table, NB * BLK, b * BLK)

        each(NB // 2, traces)
    to_scalar.wait()
    for d, out in enumerate((out0, out1, out2, out3)):
        for b in range(NB):
            for w in range(BFB):
                out[b * BFB + w : b * BFB + w + 1, :] = table[pl.ds(index[b, d * BFB + w], 1), :]


def volume_kernel(
    codes, rank, code_rows, slots, table, fields, metric, derivative, lift,
    meta, outer, curl, rows, send, place, back, lift_wide, wide, padded, order,
):
    count = 0
    for x in range(5):
        for b in range(NB):
            order[x, rank[x, b]] = b
    for b in range(NB):
        meta[b] = order[0, b]
        count += rank[5, b]
    meta[NB] = count
    for f in range(4):
        for i in range(NF):
            rows[f * NF + i : f * NF + i + 1, :] = code_rows[pl.ds(f * NB + meta[i], 1), :]
    rows[...] = compact_rows(rows[...], rank)
    for i in range(NF):
        slot = slots[pl.ds(meta[i], 1), :]
        send[i : i + 1, :] = (slot >> 10) * (NF * BLK) + i * BLK + (slot & 127)
    for d in range(4):
        for i in range(NF):
            b = order[1 + d, i]
            own = rank[0, b]
            slot = slots[pl.ds(b, 1), :]
            row = (slot >> 10) * (NF * BLK) + own * BLK + (slot & 127)
            place[d * NF + i : d * NF + i + 1, :] = jnp.where(own < NF, row, TRASH)
    wide[...] = jnp.zeros_like(wide)
    for a in range(3):
        wide[a * NPAD : a * NPAD + NP, 0:NP] = derivative[a]
    back[...] = stacked(wide[...])
    wide[0:KLIFT, :] = jnp.zeros((KLIFT, BLK), F32)
    wide[0:NP, 0:60] = lift[...]
    flat = wide[0:KLIFT, :]
    lane = lax.broadcasted_iota(jnp.int32, (KLIFT, BLK), 1)
    face_major = jnp.where(lane < 15, flat, 0.0)
    for f in range(1, 4):
        inside = (lane >= f * FPAD) & (lane < f * FPAD + 15)
        face_major = jnp.where(inside, pltpu.roll(flat, f, 1), face_major)
    hi = face_major.astype(BF16).astype(F32)
    lift_wide[:, 0:BLK] = (hi + pltpu.roll(hi, 4 * FPAD, 1)).astype(BF16)
    lift_wide[:, BLK : 2 * BLK] = (face_major - hi).astype(BF16)
    pad_nodes(fields, padded, 0, NB * BLK)

    def block(b):
        lanes = block_lanes(b)
        for f in range(4):
            copy_rows(codes, table, outer, f * NB * BLK + b * BLK)
        products = node_products(back[...], [padded[c, :, lanes] for c in range(6)])
        for c, value in enumerate(curls(products, metric, lanes)):
            curl[b, c] = value

    each(NB, block)


def full_kernel(
    slots, send, meta, table, outer_in, curl, normals, scale, medium, front, lift, in0, in1, in2, in3,
    rate, start, fine_table, out0, out1, out2, out3, outer, result, value_all, sem,
):
    for d, got in enumerate((in0, in1, in2, in3)):
        for b in range(NB):
            for w in range(BFB):
                outer[pl.ds(slots[b, d * BFB + w], 1), :] = got[b * BFB + w : b * BFB + w + 1, :]
    def copy(b):
        return pltpu.make_async_copy(result.at[b], rate.at[:, :, block_lanes(b)], sem.at[b])

    def block(b):
        lanes = block_lanes(b)
        lifted = lifted_flux(outer, table, NB * BLK, b * BLK, normals, scale, lanes, lift)
        value = tendency([curl[b, c] for c in range(6)], lifted, medium, lanes)
        for c in range(6):
            value_all[b, c] = value[c]
            result[b, c] = value[c][:NP]
        copy(b).start()

    each(NB, block)
    fine_table[ZROW : ZROW + 8, :] = jnp.zeros((8, BLK), F32)

    def fine_block(i):
        keep = i < meta[NB]
        value = [jnp.where(keep, value_all[meta[i], c], 0.0) for c in range(6)]
        for c in range(6):
            start[i, c] = value[c]
        store_traces(node_products(front[...], value), fine_table, NF * BLK, i * BLK)

    each(NF, fine_block)
    send_rows(send, fine_table, (out0, out1, out2, out3))
    for b in range(NB):
        copy(b).wait()


def fine_volume_kernel(codes, meta, table, state, metric, back, outer, curl):
    def block(i):
        for f in range(4):
            copy_rows(codes, table, outer, f * NF * BLK + i * BLK)
        products = node_products(back[...], [state[i, c] for c in range(6)])
        for c, value in enumerate(curls(products, metric, block_lanes(meta[i]))):
            curl[i, c] = value

    each(NF, block)


def fine_update(
    place, meta, state, start, table, outer, curl, normals, scale, medium, lift, ins, emit
):
    for d, got in enumerate(ins):
        for i in range(NF):
            for w in range(BFB):
                r = i * BFB + w
                outer[pl.ds(place[d * NF + i, d * BFB + w], 1), :] = got[r : r + 1, :]
    def block(i):
        lanes = block_lanes(meta[i])
        lifted = lifted_flux(outer, table, NF * BLK, i * BLK, normals, scale, lanes, lift)
        value = tendency([curl[i, c] for c in range(6)], lifted, medium, lanes)
        keep = i < meta[NB]
        emit(i, [
            jnp.where(keep, state[i, c] + start[i, c] + STEP * value[c], 0.0) for c in range(6)
        ])

    each(NF, block)


def fine_kernel(
    place, send, meta, state, start, table, outer_in, curl, normals, scale, medium, front, lift,
    in0, in1, in2, in3, new_state, new_table, out0, out1, out2, out3, outer,
):
    def emit(i, value):
        for c in range(6):
            new_state[i, c] = value[c]
        store_traces(node_products(front[...], value), new_table, NF * BLK, i * BLK)

    new_table[ZROW : ZROW + 8, :] = jnp.zeros((8, BLK), F32)
    fine_update(
        place, meta, state, start, table, outer, curl, normals, scale, medium, lift,
        (in0, in1, in2, in3), emit,
    )
    send_rows(send, new_table, (out0, out1, out2, out3))


def last_kernel(
    place, meta, state, start, table, outer_in, curl, normals, scale, medium, lift,
    in0, in1, in2, in3, rate_in, rate, outer, result, sem,
):
    def copy(i):
        return pltpu.make_async_copy(result.at[i], rate.at[:, :, block_lanes(meta[i])], sem.at[i])

    def emit(i, value):
        for c in range(6):
            result[i, c] = value[c][:NP] * 0.25

        @pl.when(i < meta[NB])
        def _():
            copy(i).start()

    fine_update(
        place, meta, state, start, table, outer, curl, normals, scale, medium, lift,
        (in0, in1, in2, in3), emit,
    )
    for i in range(NF):
        @pl.when(i < meta[NB])
        def _():
            copy(i).wait()


def fine_plan(levels):
    padded = jnp.pad(levels, ((1, 1), (1, 1), (0, 0)))
    near = lax.dynamic_slice(padded, (lax.axis_index("px"), lax.axis_index("py"), 0), (3, 3, NB))
    fine = (jnp.stack([near[1, 1], near[0, 1], near[2, 1], near[1, 0], near[1, 2]]) > 0).astype(jnp.int32)
    before = (jnp.arange(NB)[None, :] < jnp.arange(NB)[:, None]).astype(jnp.int32)
    fine_before = jnp.sum(fine[:, None, :] * before[None], axis=2)
    coarse_before = jnp.sum((1 - fine[:, None, :]) * before[None], axis=2)
    count = jnp.sum(fine, axis=1, keepdims=True)
    rank = jnp.where(fine > 0, fine_before, count + coarse_before)
    return jnp.concatenate([rank, fine[:1]])


VMEM = pl.BlockSpec(memory_space=pltpu.VMEM)
SMEM = pl.BlockSpec(memory_space=pltpu.SMEM)
HBM = pl.BlockSpec(memory_space=pltpu.HBM)
PARAMS = pltpu.CompilerParams(vmem_limit_bytes=VMEM_LIMIT)


def cost(flops, size):
    return pl.CostEstimate(flops=flops, bytes_accessed=size, transcendentals=0)


def shards(
    fields, metric, normals, face_scale, permittivity, derivative, face_interp, lift, neighbor, levels
):
    codes = neighbor.reshape(4 * NB, BLK)
    medium = permittivity.reshape(1, NB * BLK)

    def exchange(out):
        def ways(axis):
            count = lax.axis_size(axis)
            return [(i, i + 1) for i in range(count - 1)], [(i + 1, i) for i in range(count - 1)]

        x_up, x_down = ways("px")
        y_up, y_down = ways("py")
        return (
            lax.ppermute(out[1], "px", x_up),
            lax.ppermute(out[0], "px", x_down),
            lax.ppermute(out[3], "py", y_up),
            lax.ppermute(out[2], "py", y_down),
        )

    def message(rows_of):
        return [jax.ShapeDtypeStruct((rows_of, BLK), F32)] * 4

    def array(*shape, dtype=F32):
        return jax.ShapeDtypeStruct(shape, dtype)

    state_shape = array(NF, 6, NPAD, BLK)
    ranks = fine_plan(levels)
    slots, table, front, *out = pl.pallas_call(
        first_kernel,
        out_shape=[
            array(NB, BLK, dtype=jnp.int32),
            array(TAB, BLK),
            array(4 * FPAD, KROWS, dtype=BF16),
        ] + message(NB * BFB),
        in_specs=[HBM] * 3,
        out_specs=[VMEM] * 7,
        scratch_shapes=[
            pltpu.VMEM((6, NPAD, NB * BLK), F32),
            pltpu.VMEM((6, NP, NB * BLK), F32),
            pltpu.VMEM((4 * NB, BLK), jnp.int32),
            pltpu.VMEM((15, 4, NP), F32),
            pltpu.VMEM((BLK, BLK), F32),
            pltpu.SMEM((NB, BLK), jnp.int32),
            pltpu.SemaphoreType.DMA((5,)),
        ],
        compiler_params=PARAMS,
        cost_estimate=cost(10**9, 2 * 10**6),
        name="border",
    )(codes, fields, face_interp.transpose(1, 0, 2))
    received = exchange(out)
    meta, outer, curl, rows, send, place, back, lift_wide = pl.pallas_call(
        volume_kernel,
        out_shape=[
            array(NB + 1, dtype=jnp.int32),
            array(SLOTS, BLK),
            array(NB, 6, NPAD, BLK),
            array(4 * NF, BLK, dtype=jnp.int32),
            array(NF, BLK, dtype=jnp.int32),
            array(4 * NF, BLK, dtype=jnp.int32),
            array(BLK, KROWS, dtype=BF16),
            array(KLIFT, 2 * BLK, dtype=BF16),
        ],
        in_specs=[SMEM] * 2 + [VMEM] * 7,
        out_specs=[SMEM] + [VMEM] * 7,
        scratch_shapes=[
            pltpu.VMEM((BLK, BLK), F32),
            pltpu.VMEM((6, NPAD, NB * BLK), F32),
            pltpu.SMEM((5, NB), jnp.int32),
        ],
        compiler_params=PARAMS,
        cost_estimate=cost(10**9, 4 * 10**6),
        name="volume",
    )(neighbor.reshape(SLOTS), ranks, codes, slots, table, fields, metric, derivative, lift)
    rows = rows.reshape(FSLOTS)
    rate, start, table, *out = pl.pallas_call(
        full_kernel,
        out_shape=[array(6, NP, NB * BLK), state_shape, array(FTAB, BLK)] + message(NF * BFB) + [array(SLOTS, BLK)],
        in_specs=[SMEM] * 3 + [VMEM] * 12,
        out_specs=[HBM] + [VMEM] * 7,
        scratch_shapes=[
            pltpu.VMEM((NB, 6, NP, BLK), F32),
            pltpu.VMEM((NB, 6, NPAD, BLK), F32),
            pltpu.SemaphoreType.DMA((NB,)),
        ],
        input_output_aliases={4: 7},
        compiler_params=PARAMS,
        cost_estimate=cost(10**9, 4 * 10**6),
        name="full",
    )(slots, send, meta, table, outer, curl, normals, face_scale, medium, front, lift_wide, *received)
    state = start
    for step in range(3):
        received = exchange(out)
        outer, curl = pl.pallas_call(
            fine_volume_kernel,
            out_shape=[array(FSLOTS + 8, BLK), state_shape],
            in_specs=[SMEM] * 2 + [VMEM] * 4,
            out_specs=[VMEM] * 2,
            compiler_params=PARAMS,
            cost_estimate=cost(10**9, 2 * 10**6),
            name="fine_volume",
        )(rows, meta, table, state, metric, back)
        geometry = (normals, face_scale, medium)
        if step < 2:
            state, table, *out = pl.pallas_call(
                fine_kernel,
                out_shape=[state_shape, array(FTAB, BLK)] + message(NF * BFB) + [array(FSLOTS + 8, BLK)],
                in_specs=[SMEM] * 3 + [VMEM] * 14,
                out_specs=[VMEM] * 7,
                input_output_aliases={6: 6},
                compiler_params=PARAMS,
                cost_estimate=cost(10**9, 2 * 10**6),
                name="fine",
            )(place, send, meta, state, start, table, outer, curl, *geometry, front, lift_wide, *received)
    return pl.pallas_call(
        last_kernel,
        out_shape=[array(6, NP, NB * BLK), array(FSLOTS + 8, BLK)],
        in_specs=[SMEM] * 2 + [VMEM] * 13 + [HBM],
        out_specs=[HBM, VMEM],
        scratch_shapes=[pltpu.VMEM((NF, 6, NP, BLK), F32), pltpu.SemaphoreType.DMA((NF,))],
        input_output_aliases={15: 0, 5: 1},
        compiler_params=PARAMS,
        cost_estimate=cost(10**9, 2 * 10**6),
        name="last",
    )(place, meta, state, start, table, outer, curl, *geometry, lift_wide, *received, rate)[0]


def solution(mesh):
    in_specs = (
        P(None, None, ("px", "py")),
        P(None, None, ("px", "py")),
        P(None, None, ("px", "py")),
        P(None, ("px", "py")),
        P(("px", "py")),
        P(),
        P(),
        P(),
        P("px", "py", None),
        P(),
    )
    out_specs = P(None, None, ("px", "py"))
    return jax.shard_map(shards, mesh=mesh, in_specs=in_specs, out_specs=out_specs, check_vma=False)
```

time: 103 us -> 95 us (0.922)
  waiting for transfers between devices: 18.1 us -> 8.68 us
  Pallas kernels: 22.7 us -> 24.5 us
  starting transfers between devices: 54.3 us -> 55.9 us
  other arithmetic: 1.69 us -> 0.45 us
    ppermute x4, waiting for transfers between devices: 17.3 us -> 8.65 us  [exchange(): lax.ppermute(out[2], 'py', y_down)]
    pallas_call x5 -> x9, Pallas kernels: 22.7 us -> 24.5 us  [the longest x3 6.15 us: shards(): pl.pallas_call(fine_volume_kernel, out_shape=[array(FSLOTS + 8, BLK), sta...]
    ppermute x4, starting transfers between devices: 18.3 us -> 19.8 us  [exchange(): lax.ppermute(out[3], 'py', y_up)]
  transfers between devices with their start and end apart: 16 -> 16, of which waited for: 7 -> 3; matrix products, arithmetic and copies ran while one was open for 2% -> 1% of each run, Pallas kernels for 0% -> 11%
where the time goes in v1:
time: 95 us; the launch traced here: 94.3 us
  starting transfers between devices  55.9 us (59%)
  Pallas kernels  24.5 us (26%)
  waiting for transfers between devices  8.68 us (9%)
  local copies, waits for them, and re-layouts  4.2 us (4%)
    ppermute x4, starting transfers between devices, exchange(): lax.ppermute(out[0], 'px', x_down)  23 us
    ppermute x4, starting transfers between devices, exchange(): lax.ppermute(out[3], 'py', y_up)  19.8 us
    ppermute x4, waiting for transfers between devices, exchange(): lax.ppermute(out[2], 'py', y_down)  8.65 us
    ppermute x4, starting transfers between devices, exchange(): lax.ppermute(out[1], 'px', x_up)  7.68 us
    pallas_call x3, Pallas kernels, shards(): pl.pallas_call(fine_volume_kernel, out_shape=[array(FSLOTS + 8, BLK), sta...  6.15 us
    ppermute x4, starting transfers between devices, exchange(): lax.ppermute(out[2], 'py', y_down)  5.35 us
    pallas_call x2, Pallas kernels, shards(): pl.pallas_call(fine_kernel, out_shape=[state_shape, array(FTAB, BLK)] + m...  4.58 us
    pallas_call x1, Pallas kernels, shards(): pl.pallas_call(full_kernel, out_shape=[array(6, NP, NB * BLK), state_shap...  4.4 us
  transfers between devices with their start and end apart: 16, of which 3 were waited for; matrix products, arithmetic and copies ran while one was open for 1% of the time, Pallas kernels for 11%

profile of v1, /device:TPU:6, one launch (start us, length us, event | category | flops | bytes accessed | tf_op | source)
XLA Modules:
  0.0 94.3 jit_solution(2024969220541005852)
XLA Ops:
  2.7 2.4 %border.1 = (s32[8,128]{1,0:T(8,128)S(1)}, f32[4608,128]{1,0:T(8,128)S(1)}, bf16[64,128]{1,0:T(8,128)(2,1)S(1)}, f32[128,128]{1,0:T(8,128)S(1)}, f32[128,128]{1,...) custom-call(s32[32,128]{1,0:T(8,128)S(1)} %bitcast.15, f32[6,35,1024]{2,1,0:T(8,128)S(1)} %copy-done.3, ...), custom_call_target="tpu_custom_call" | custom-call | flops 1000000000 | bytes 2000000 | tf_op jit(solution)/shard_map/border/pallas_call | solution.py:413
  5.1 1.9 %collective-permute-start = (f32[128,128]{1,0:T(8,128)S(1)}, f32[128,128]{1,0:T(8,128)S(1)}, u32[]{:S(2)}, u32[]{:S(2)}) collective-permute-start(f32[128,128]{1,0:T(8,128)S(1)} %get-tuple-element.55), channel_id=1, source_target_pairs={{0,12},{12,24},{24,36},{36,48},{48,60},{60,72},{72,84},{84,96},{96... | collective-permute-start | bytes 196616 | tf_op jit(solution)/shard_map/ppermute | solution.py:399
  7.1 5.8 %collective-permute-start.1 = (f32[128,128]{1,0:T(8,128)S(1)}, f32[128,128]{1,0:T(8,128)S(1)}, u32[]{:S(2)}, u32[]{:S(2)}) collective-permute-start(f32[128,128]{1,0:T(8,128)S(1)} %get-tuple-element.56), channel_id=1, source_target_pairs={{12,0},{24,12},{36,24},{48,36},{60,48},{72,60},{84,72},{96,84},{10... | collective-permute-start | bytes 196616 | tf_op jit(solution)/shard_map/ppermute | solution.py:400
  12.8 4.3 %collective-permute-start.2 = (f32[128,128]{1,0:T(8,128)S(1)}, f32[128,128]{1,0:T(8,128)S(1)}, u32[]{:S(2)}, u32[]{:S(2)}) collective-permute-start(f32[128,128]{1,0:T(8,128)S(1)} %get-tuple-element.57), channel_id=1, source_target_pairs={{0,1},{1,2},{2,3},{3,4},{4,5},{5,6},{6,7},{7,8},{8,9},{9,10},{10,1... | collective-permute-start | bytes 196616 | tf_op jit(solution)/shard_map/ppermute | solution.py:401
  20.5 4.2 %volume.1 = (s32[9]{0:T(128)S(1)}, f32[4096,128]{1,0:T(8,128)S(1)}, f32[8,6,40,128]{3,2,1,0:T(8,128)S(1)}, s32[16,128]{1,0:T(8,128)S(1)}, s32[4,128]{1,0:T(4,128...) custom-call(s32[4096]{0:T(1024)S(1)} %bitcast.16, ...), custom_call_target="tpu_custom_call" | custom-call | flops 1000000000 | bytes 4000000 | tf_op jit(solution)/shard_map/volume/pallas_call | solution.py:436
  24.7 4.4 %full.1 = (f32[6,35,1024]{2,1,0:T(8,128)}, f32[4,6,40,128]{3,2,1,0:T(8,128)S(1)}, f32[2056,128]{1,0:T(8,128)S(1)}, f32[64,128]{1,0:T(8,128)S(1)}, f32[64,128]{1,...) custom-call(s32[8,128]{1,0:T(8,128)S(1)} %get-tuple-element.46.slots, ...), custom_call_target="tpu_custom_call", output_to_operand_aliasing={{7}: (4, {})} | custom-call | flops 1000000000 | bytes 4000000 | tf_op jit(solution)/shard_map/full/pallas_call | solution.py:460
  29.1 1.9 %collective-permute-start.4 = (f32[64,128]{1,0:T(8,128)S(1)}, f32[64,128]{1,0:T(8,128)S(1)}, u32[]{:S(2)}, u32[]{:S(2)}) collective-permute-start(f32[64,128]{1,0:T(8,128)S(1)} %get-tuple-element.65), channel_id=1, source_target_pairs={{0,12},{12,24},{24,36},{36,48},{48,60},{60,72},{72,84},{84,96},{96... | collective-permute-start | bytes 98312 | tf_op jit(solution)/shard_map/ppermute | solution.py:399
  31.1 5.8 %collective-permute-start.5 = (f32[64,128]{1,0:T(8,128)S(1)}, f32[64,128]{1,0:T(8,128)S(1)}, u32[]{:S(2)}, u32[]{:S(2)}) collective-permute-start(f32[64,128]{1,0:T(8,128)S(1)} %get-tuple-element.66), channel_id=1, source_target_pairs={{12,0},{24,12},{36,24},{48,36},{60,48},{72,60},{84,72},{96,84},{10... | collective-permute-start | bytes 98312 | tf_op jit(solution)/shard_map/ppermute | solution.py:400
  36.8 4.9 %collective-permute-start.6 = (f32[64,128]{1,0:T(8,128)S(1)}, f32[64,128]{1,0:T(8,128)S(1)}, u32[]{:S(2)}, u32[]{:S(2)}) collective-permute-start(f32[64,128]{1,0:T(8,128)S(1)} %get-tuple-element.67), channel_id=1, source_target_pairs={{0,1},{1,2},{2,3},{3,4},{4,5},{5,6},{6,7},{7,8},{8,9},{9,10},{10,1... | collective-permute-start | bytes 98312 | tf_op jit(solution)/shard_map/ppermute | solution.py:401
  43.0 2.1 %fine_volume.3 = (f32[2056,128]{1,0:T(8,128)S(1)}, f32[4,6,40,128]{3,2,1,0:T(8,128)S(1)}) custom-call(s32[2048]{0:T(1024)S(1)} %bitcast.18, s32[9]{0:T(128)S(1)} %get-tuple-element.49.meta, f32[2056,128]{1,0:T(8,128)S(1)} %get-tuple-element.60.table, f32[4,6,40,128]{3,2,1,0:T(8,128)S(1)} %get-tuple-element.59.state.start, f32[3,3,1024]{2,1,0:T(4,128)S(1)} %copy-done.6, ...), custom_call_target="tpu_custom_call" | custom-call | flops 1000000000 | bytes 2000000 | tf_op jit(solution)/shard_map/fine_volume/pallas_call | solution.py:478
  45.1 2.8 %collective-permute-done.7.in3 = f32[64,128]{1,0:T(8,128)S(1)} collective-permute-done((f32[64,128]{1,0:T(8,128)S(1)}, f32[64,128]{1,0:T(8,128)S(1)}, u32[]{:S(2)}, u32[]{:S(2)}) %collective-permute-start.7) | collective-permute-done | bytes 32800 | tf_op jit(solution)/shard_map/ppermute | solution.py:402
  47.9 2.3 %fine.2 = (f32[4,6,40,128]{3,2,1,0:T(8,128)S(1)}, f32[2056,128]{1,0:T(8,128)S(1)}, f32[64,128]{1,0:T(8,128)S(1)}, f32[64,128]{1,0:T(8,128)S(1)}, f32[64,128]{1,0...) custom-call(s32[16,128]{1,0:T(8,128)S(1)} %get-tuple-element.48.place, ...), custom_call_target="tpu_custom_call", output_to_operand_aliasing={{6}: (6, {})} | custom-call | flops 1000000000 | bytes 2000000 | tf_op jit(solution)/shard_map/fine/pallas_call | solution.py:489
  50.2 1.9 %collective-permute-start.8 = (f32[64,128]{1,0:T(8,128)S(1)}, f32[64,128]{1,0:T(8,128)S(1)}, u32[]{:S(2)}, u32[]{:S(2)}) collective-permute-start(f32[64,128]{1,0:T(8,128)S(1)} %get-tuple-element.73), channel_id=1, source_target_pairs={{0,12},{12,24},{24,36},{36,48},{48,60},{60,72},{72,84},{84,96},{96... | collective-permute-start | bytes 98312 | tf_op jit(solution)/shard_map/ppermute | solution.py:399
  52.1 5.8 %collective-permute-start.9 = (f32[64,128]{1,0:T(8,128)S(1)}, f32[64,128]{1,0:T(8,128)S(1)}, u32[]{:S(2)}, u32[]{:S(2)}) collective-permute-start(f32[64,128]{1,0:T(8,128)S(1)} %get-tuple-element.74), channel_id=1, source_target_pairs={{12,0},{24,12},{36,24},{48,36},{60,48},{72,60},{84,72},{96,84},{10... | collective-permute-start | bytes 98312 | tf_op jit(solution)/shard_map/ppermute | solution.py:400
  57.9 5.5 %collective-permute-start.10 = (f32[64,128]{1,0:T(8,128)S(1)}, f32[64,128]{1,0:T(8,128)S(1)}, u32[]{:S(2)}, u32[]{:S(2)}) collective-permute-start(f32[64,128]{1,0:T(8,128)S(1)} %get-tuple-element.75), channel_id=1, source_target_pairs={{0,1},{1,2},{2,3},{3,4},{4,5},{5,6},{6,7},{7,8},{8,9},{9,10},{10,1... | collective-permute-start | bytes 98312 | tf_op jit(solution)/shard_map/ppermute | solution.py:401
  64.9 2.0 %fine_volume.4 = (f32[2056,128]{1,0:T(8,128)S(1)}, f32[4,6,40,128]{3,2,1,0:T(8,128)S(1)}) custom-call(s32[2048]{0:T(1024)S(1)} %bitcast.19, s32[9]{0:T(128)S(1)} %get-tuple-element.49.meta, f32[2056,128]{1,0:T(8,128)S(1)} %get-tuple-element.70.table, f32[4,6,40,128]{3,2,1,0:T(8,128)S(1)} %get-tuple-element.69.state, f32[3,3,1024]{2,1,0:T(4,128)S(1)} %copy-done.6, ...), custom_call_target="tpu_custom_call" | custom-call | flops 1000000000 | bytes 2000000 | tf_op jit(solution)/shard_map/fine_volume/pallas_call | solution.py:478
  67.0 3.5 %collective-permute-done.11.in3 = f32[64,128]{1,0:T(8,128)S(1)} collective-permute-done((f32[64,128]{1,0:T(8,128)S(1)}, f32[64,128]{1,0:T(8,128)S(1)}, u32[]{:S(2)}, u32[]{:S(2)}) %collective-permute-start.11) | collective-permute-done | bytes 32800 | tf_op jit(solution)/shard_map/ppermute | solution.py:402
  70.4 2.3 %fine.3 = (f32[4,6,40,128]{3,2,1,0:T(8,128)S(1)}, f32[2056,128]{1,0:T(8,128)S(1)}, f32[64,128]{1,0:T(8,128)S(1)}, f32[64,128]{1,0:T(8,128)S(1)}, f32[64,128]{1,0...) custom-call(s32[16,128]{1,0:T(8,128)S(1)} %get-tuple-element.48.place, ...), custom_call_target="tpu_custom_call", output_to_operand_aliasing={{6}: (6, {})} | custom-call | flops 1000000000 | bytes 2000000 | tf_op jit(solution)/shard_map/fine/pallas_call | solution.py:489
  72.7 1.9 %collective-permute-start.12 = (f32[64,128]{1,0:T(8,128)S(1)}, f32[64,128]{1,0:T(8,128)S(1)}, u32[]{:S(2)}, u32[]{:S(2)}) collective-permute-start(f32[64,128]{1,0:T(8,128)S(1)} %get-tuple-element.81), channel_id=1, source_target_pairs={{0,12},{12,24},{24,36},{36,48},{48,60},{60,72},{72,84},{84,96},{96... | collective-permute-start | bytes 98312 | tf_op jit(solution)/shard_map/ppermute | solution.py:399
  74.6 5.8 %collective-permute-start.13 = (f32[64,128]{1,0:T(8,128)S(1)}, f32[64,128]{1,0:T(8,128)S(1)}, u32[]{:S(2)}, u32[]{:S(2)}) collective-permute-start(f32[64,128]{1,0:T(8,128)S(1)} %get-tuple-element.82), channel_id=1, source_target_pairs={{12,0},{24,12},{36,24},{48,36},{60,48},{72,60},{84,72},{96,84},{10... | collective-permute-start | bytes 98312 | tf_op jit(solution)/shard_map/ppermute | solution.py:400
  80.4 5.1 %collective-permute-start.14 = (f32[64,128]{1,0:T(8,128)S(1)}, f32[64,128]{1,0:T(8,128)S(1)}, u32[]{:S(2)}, u32[]{:S(2)}) collective-permute-start(f32[64,128]{1,0:T(8,128)S(1)} %get-tuple-element.83), channel_id=1, source_target_pairs={{0,1},{1,2},{2,3},{3,4},{4,5},{5,6},{6,7},{7,8},{8,9},{9,10},{10,1... | collective-permute-start | bytes 98312 | tf_op jit(solution)/shard_map/ppermute | solution.py:401
  86.8 2.1 %fine_volume.5 = (f32[2056,128]{1,0:T(8,128)S(1)}, f32[4,6,40,128]{3,2,1,0:T(8,128)S(1)}) custom-call(s32[2048]{0:T(1024)S(1)} %bitcast.20, s32[9]{0:T(128)S(1)} %get-tuple-element.49.meta, f32[2056,128]{1,0:T(8,128)S(1)} %get-tuple-element.78.table, f32[4,6,40,128]{3,2,1,0:T(8,128)S(1)} %get-tuple-element.77.state, f32[3,3,1024]{2,1,0:T(4,128)S(1)} %copy-done.6, ...), custom_call_target="tpu_custom_call" | custom-call | flops 1000000000 | bytes 2000000 | tf_op jit(solution)/shard_map/fine_volume/pallas_call | solution.py:478
  88.9 2.4 %collective-permute-done.15.in3 = f32[64,128]{1,0:T(8,128)S(1)} collective-permute-done((f32[64,128]{1,0:T(8,128)S(1)}, f32[64,128]{1,0:T(8,128)S(1)}, u32[]{:S(2)}, u32[]{:S(2)}) %collective-permute-start.15) | collective-permute-done | bytes 32800 | tf_op jit(solution)/shard_map/ppermute | solution.py:402
  91.3 2.8 %last.1 = (f32[6,35,1024]{2,1,0:T(8,128)}, f32[2056,128]{1,0:T(8,128)S(1)}) custom-call(s32[16,128]{1,0:T(8,128)S(1)} %get-tuple-element.48.place, s32[9]{0:T(128)S(1)} %get-tuple-element.49.meta, f32[4,6,40,128]{3,2,1,0:T(8,128)S(1)} %get-tuple-element.77.state, ...), custom_call_target="tpu_custom_call", output_to_operand_aliasing={{0}: (15, {}), {1}: (5, {})} | custom-call | flops 1000000000 | bytes 2000000 | tf_op jit(solution)/shard_map/last/pallas_call | solution.py:499
  (51 shorter events, 10.0 us)
Async XLA Ops:
  2.7 15.8 %copy-start.11 = (s32[64,12,8]{0,2,1:T(8,128)S(1)}, s32[64,12,8]{0,2,1:T(8,128)}, u32[]{:S(2)}) copy-start(s32[64,12,8]{0,2,1:T(8,128)} %param.19) | copy-start | bytes 73732
  2.7 16.6 %copy-start.5 = (f32[3,35,35]{2,1,0:T(8,128)S(1)}, f32[3,35,35]{2,1,0:T(8,128)}, u32[]{:S(2)}) copy-start(f32[3,35,35]{2,1,0:T(8,128)} %derivative.1) | copy-start | bytes 44104
  2.7 16.6 %copy-start.6 = (f32[3,3,1024]{2,1,0:T(4,128)S(1)}, f32[3,3,1024]{2,1,0:T(4,128)}, u32[]{:S(2)}) copy-start(f32[3,3,1024]{2,1,0:T(4,128)} %metric.7) | copy-start | bytes 110596
  2.7 16.6 %copy-start.8 = (f32[35,60]{1,0:T(8,128)S(1)}, f32[35,60]{1,0:T(8,128)}, u32[]{:S(2)}) copy-start(f32[35,60]{1,0:T(8,128)} %lift.1) | copy-start | bytes 25204
  2.7 16.6 %copy-start.10 = (s32[1,1,4096]{2,1,0:T(1,128)S(1)}, s32[1,1,4096]{2,1,0:T(1,128)}, u32[]{:S(2)}) copy-start(s32[1,1,4096]{2,1,0:T(1,128)} %param.18) | copy-start | bytes 49156
  5.1 19.5 %collective-permute-start = (f32[128,128]{1,0:T(8,128)S(1)}, f32[128,128]{1,0:T(8,128)S(1)}, u32[]{:S(2)}, u32[]{:S(2)}) collective-permute-start(f32[128,128]{1,0:T(8,128)S(1)} %get-tuple-element.55), channel_id=1, source_target_pairs={{0,12},{12,24},{24,36},{36,48},{48,60},{60,72},{72,84},{84,96},{96... | collective-permute-start | bytes 196616 | tf_op jit(solution)/shard_map/ppermute | solution.py:399
  7.1 17.6 %collective-permute-start.1 = (f32[128,128]{1,0:T(8,128)S(1)}, f32[128,128]{1,0:T(8,128)S(1)}, u32[]{:S(2)}, u32[]{:S(2)}) collective-permute-start(f32[128,128]{1,0:T(8,128)S(1)} %get-tuple-element.56), channel_id=1, source_target_pairs={{12,0},{24,12},{36,24},{48,36},{60,48},{72,60},{84,72},{96,84},{10... | collective-permute-start | bytes 196616 | tf_op jit(solution)/shard_map/ppermute | solution.py:400
  12.8 11.9 %collective-permute-start.2 = (f32[128,128]{1,0:T(8,128)S(1)}, f32[128,128]{1,0:T(8,128)S(1)}, u32[]{:S(2)}, u32[]{:S(2)}) collective-permute-start(f32[128,128]{1,0:T(8,128)S(1)} %get-tuple-element.57), channel_id=1, source_target_pairs={{0,1},{1,2},{2,3},{3,4},{4,5},{5,6},{6,7},{7,8},{8,9},{9,10},{10,1... | collective-permute-start | bytes 196616 | tf_op jit(solution)/shard_map/ppermute | solution.py:401
  17.1 7.6 %collective-permute-start.3 = (f32[128,128]{1,0:T(8,128)S(1)}, f32[128,128]{1,0:T(8,128)S(1)}, u32[]{:S(2)}, u32[]{:S(2)}) collective-permute-start(f32[128,128]{1,0:T(8,128)S(1)} %get-tuple-element.58), channel_id=1, source_target_pairs={{1,0},{2,1},{3,2},{4,3},{5,4},{6,5},{7,6},{8,7},{9,8},{10,9},{11,1... | collective-permute-start | bytes 196616 | tf_op jit(solution)/shard_map/ppermute | solution.py:402
  20.5 4.2 %copy-start = (f32[3,4,1024]{2,1,0:T(4,128)S(1)}, f32[3,4,1024]{2,1,0:T(4,128)}, u32[]{:S(2)}) copy-start(f32[3,4,1024]{2,1,0:T(4,128)} %normals.7) | copy-start | bytes 147460
  20.5 4.2 %copy-start.1 = (f32[4,1024]{1,0:T(4,128)S(1)}, f32[4,1024]{1,0:T(4,128)}, u32[]{:S(2)}) copy-start(f32[4,1024]{1,0:T(4,128)} %scale.7) | copy-start | bytes 49156
  20.5 4.2 %copy-start.2 = (f32[1024]{0:T(1024)S(1)}, f32[1024]{0:T(1024)}, u32[]{:S(2)}) copy-start(f32[1024]{0:T(1024)} %param.14) | copy-start | bytes 12292
  29.1 16.0 %collective-permute-start.4 = (f32[64,128]{1,0:T(8,128)S(1)}, f32[64,128]{1,0:T(8,128)S(1)}, u32[]{:S(2)}, u32[]{:S(2)}) collective-permute-start(f32[64,128]{1,0:T(8,128)S(1)} %get-tuple-element.65), channel_id=1, source_target_pairs={{0,12},{12,24},{24,36},{36,48},{48,60},{60,72},{72,84},{84,96},{96... | collective-permute-start | bytes 98312 | tf_op jit(solution)/shard_map/ppermute | solution.py:399
  31.1 14.0 %collective-permute-start.5 = (f32[64,128]{1,0:T(8,128)S(1)}, f32[64,128]{1,0:T(8,128)S(1)}, u32[]{:S(2)}, u32[]{:S(2)}) collective-permute-start(f32[64,128]{1,0:T(8,128)S(1)} %get-tuple-element.66), channel_id=1, source_target_pairs={{12,0},{24,12},{36,24},{48,36},{60,48},{72,60},{84,72},{96,84},{10... | collective-permute-start | bytes 98312 | tf_op jit(solution)/shard_map/ppermute | solution.py:400
  36.8 8.3 %collective-permute-start.6 = (f32[64,128]{1,0:T(8,128)S(1)}, f32[64,128]{1,0:T(8,128)S(1)}, u32[]{:S(2)}, u32[]{:S(2)}) collective-permute-start(f32[64,128]{1,0:T(8,128)S(1)} %get-tuple-element.67), channel_id=1, source_target_pairs={{0,1},{1,2},{2,3},{3,4},{4,5},{5,6},{6,7},{7,8},{8,9},{9,10},{10,1... | collective-permute-start | bytes 98312 | tf_op jit(solution)/shard_map/ppermute | solution.py:401
  41.7 6.2 %collective-permute-start.7 = (f32[64,128]{1,0:T(8,128)S(1)}, f32[64,128]{1,0:T(8,128)S(1)}, u32[]{:S(2)}, u32[]{:S(2)}) collective-permute-start(f32[64,128]{1,0:T(8,128)S(1)} %get-tuple-element.68), channel_id=1, source_target_pairs={{1,0},{2,1},{3,2},{4,3},{5,4},{6,5},{7,6},{8,7},{9,8},{10,9},{11,1... | collective-permute-start | bytes 98312 | tf_op jit(solution)/shard_map/ppermute | solution.py:402
  50.2 16.7 %collective-permute-start.8 = (f32[64,128]{1,0:T(8,128)S(1)}, f32[64,128]{1,0:T(8,128)S(1)}, u32[]{:S(2)}, u32[]{:S(2)}) collective-permute-start(f32[64,128]{1,0:T(8,128)S(1)} %get-tuple-element.73), channel_id=1, source_target_pairs={{0,12},{12,24},{24,36},{36,48},{48,60},{60,72},{72,84},{84,96},{96... | collective-permute-start | bytes 98312 | tf_op jit(solution)/shard_map/ppermute | solution.py:399
  52.1 14.8 %collective-permute-start.9 = (f32[64,128]{1,0:T(8,128)S(1)}, f32[64,128]{1,0:T(8,128)S(1)}, u32[]{:S(2)}, u32[]{:S(2)}) collective-permute-start(f32[64,128]{1,0:T(8,128)S(1)} %get-tuple-element.74), channel_id=1, source_target_pairs={{12,0},{24,12},{36,24},{48,36},{60,48},{72,60},{84,72},{96,84},{10... | collective-permute-start | bytes 98312 | tf_op jit(solution)/shard_map/ppermute | solution.py:400
  57.9 9.1 %collective-permute-start.10 = (f32[64,128]{1,0:T(8,128)S(1)}, f32[64,128]{1,0:T(8,128)S(1)}, u32[]{:S(2)}, u32[]{:S(2)}) collective-permute-start(f32[64,128]{1,0:T(8,128)S(1)} %get-tuple-element.75), channel_id=1, source_target_pairs={{0,1},{1,2},{2,3},{3,4},{4,5},{5,6},{6,7},{7,8},{8,9},{9,10},{10,1... | collective-permute-start | bytes 98312 | tf_op jit(solution)/shard_map/ppermute | solution.py:401
  63.4 7.0 %collective-permute-start.11 = (f32[64,128]{1,0:T(8,128)S(1)}, f32[64,128]{1,0:T(8,128)S(1)}, u32[]{:S(2)}, u32[]{:S(2)}) collective-permute-start(f32[64,128]{1,0:T(8,128)S(1)} %get-tuple-element.76), channel_id=1, source_target_pairs={{1,0},{2,1},{3,2},{4,3},{5,4},{6,5},{7,6},{8,7},{9,8},{10,9},{11,1... | collective-permute-start | bytes 98312 | tf_op jit(solution)/shard_map/ppermute | solution.py:402
  72.7 16.2 %collective-permute-start.12 = (f32[64,128]{1,0:T(8,128)S(1)}, f32[64,128]{1,0:T(8,128)S(1)}, u32[]{:S(2)}, u32[]{:S(2)}) collective-permute-start(f32[64,128]{1,0:T(8,128)S(1)} %get-tuple-element.81), channel_id=1, source_target_pairs={{0,12},{12,24},{24,36},{36,48},{48,60},{60,72},{72,84},{84,96},{96... | collective-permute-start | bytes 98312 | tf_op jit(solution)/shard_map/ppermute | solution.py:399
  74.6 14.3 %collective-permute-start.13 = (f32[64,128]{1,0:T(8,128)S(1)}, f32[64,128]{1,0:T(8,128)S(1)}, u32[]{:S(2)}, u32[]{:S(2)}) collective-permute-start(f32[64,128]{1,0:T(8,128)S(1)} %get-tuple-element.82), channel_id=1, source_target_pairs={{12,0},{24,12},{36,24},{48,36},{60,48},{72,60},{84,72},{96,84},{10... | collective-permute-start | bytes 98312 | tf_op jit(solution)/shard_map/ppermute | solution.py:400
  80.4 8.5 %collective-permute-start.14 = (f32[64,128]{1,0:T(8,128)S(1)}, f32[64,128]{1,0:T(8,128)S(1)}, u32[]{:S(2)}, u32[]{:S(2)}) collective-permute-start(f32[64,128]{1,0:T(8,128)S(1)} %get-tuple-element.83), channel_id=1, source_target_pairs={{0,1},{1,2},{2,3},{3,4},{4,5},{5,6},{6,7},{7,8},{8,9},{9,10},{10,1... | collective-permute-start | bytes 98312 | tf_op jit(solution)/shard_map/ppermute | solution.py:401
  85.5 5.8 %collective-permute-start.15 = (f32[64,128]{1,0:T(8,128)S(1)}, f32[64,128]{1,0:T(8,128)S(1)}, u32[]{:S(2)}, u32[]{:S(2)}) collective-permute-start(f32[64,128]{1,0:T(8,128)S(1)} %get-tuple-element.84), channel_id=1, source_target_pairs={{1,0},{2,1},{3,2},{4,3},{5,4},{6,5},{7,6},{8,7},{9,8},{10,9},{11,1... | collective-permute-start | bytes 98312 | tf_op jit(solution)/shard_map/ppermute | solution.py:402
  (4 other events, 3.9 us)

commit v2 on v1

--- a/solution.py
+++ b/solution.py
@@ -153,7 +153,7 @@
 
 
 def first_kernel(
-    code_rows, fields, interp, slots, table, front, out0, out1, out2, out3,
+    ranks, code_rows, fields, interp, slots, table, front, out0, out1, out2, out3,
     padded, raw, code_buf, interp_buf, wide, index, sem,
 ):
     half = NB * BLK // 2
@@ -251,40 +251,49 @@
     each(NB, block)
 
 
+def start_rate(b, outer, table, curl, normals, scale, medium, lift):
+    lanes = block_lanes(b)
+    lifted = lifted_flux(
+        outer, table, NB * BLK, pl.multiple_of(b * BLK, BLK), normals, scale, lanes, lift
+    )
+    return tendency([curl[b, c] for c in range(6)], lifted, medium, lanes)
+
+
 def full_kernel(
     slots, send, meta, table, outer_in, curl, normals, scale, medium, front, lift, in0, in1, in2, in3,
-    rate, start, fine_table, out0, out1, out2, out3, outer, result, value_all, sem,
+    start, state, fine_table, out0, out1, out2, out3, outer,
 ):
     for d, got in enumerate((in0, in1, in2, in3)):
         for b in range(NB):
             for w in range(BFB):
                 outer[pl.ds(slots[b, d * BFB + w], 1), :] = got[b * BFB + w : b * BFB + w + 1, :]
-    def copy(b):
-        return pltpu.make_async_copy(result.at[b], rate.at[:, :, block_lanes(b)], sem.at[b])
-
-    def block(b):
-        lanes = block_lanes(b)
-        lifted = lifted_flux(outer, table, NB * BLK, b * BLK, normals, scale, lanes, lift)
-        value = tendency([curl[b, c] for c in range(6)], lifted, medium, lanes)
-        for c in range(6):
-            value_all[b, c] = value[c]
-            result[b, c] = value[c][:NP]
-        copy(b).start()
-
-    each(NB, block)
     fine_table[ZROW : ZROW + 8, :] = jnp.zeros((8, BLK), F32)
-
-    def fine_block(i):
+    for i in range(NF):
+        value = start_rate(meta[i], outer, table, curl, normals, scale, medium, lift)
         keep = i < meta[NB]
-        value = [jnp.where(keep, value_all[meta[i], c], 0.0) for c in range(6)]
+        kept = [jnp.where(keep, x, 0.0) for x in value]
         for c in range(6):
             start[i, c] = value[c]
-        store_traces(node_products(front[...], value), fine_table, NF * BLK, i * BLK)
-
-    each(NF, fine_block)
+            state[i, c] = kept[c]
+        store_traces(node_products(front[...], kept), fine_table, NF * BLK, i * BLK)
     send_rows(send, fine_table, (out0, out1, out2, out3))
-    for b in range(NB):
-        copy(b).wait()
+
+
+def coarse_kernel(
+    codes, meta, table, state, metric, back, all_outer, all_table, all_curl, normals, scale, medium, lift,
+    outer, curl, rate, result, sem,
+):
+    copies = []
+    for j in range(NB - NF):
+        b = meta[NF + j]
+        value = start_rate(b, all_outer, all_table, all_curl, normals, scale, medium, lift)
+        for c in range(6):
+            result[j, c] = value[c][:NP]
+        copies.append(pltpu.make_async_copy(result.at[j], rate.at[:, :, block_lanes(b)], sem.at[j]))
+        copies[-1].start()
+    fine_volume_kernel(codes, meta, table, state, metric, back, outer, curl)
+    for copy in copies:
+        copy.wait()
 
 
 def fine_volume_kernel(codes, meta, table, state, metric, back, outer, curl):
@@ -343,21 +352,17 @@
         return pltpu.make_async_copy(result.at[i], rate.at[:, :, block_lanes(meta[i])], sem.at[i])
 
     def emit(i, value):
+        keep = i < meta[NB]
         for c in range(6):
-            result[i, c] = value[c][:NP] * 0.25
-
-        @pl.when(i < meta[NB])
-        def _():
-            copy(i).start()
+            result[i, c] = jnp.where(keep, value[c] * 0.25, start[i, c])[:NP]
+        copy(i).start()
 
     fine_update(
         place, meta, state, start, table, outer, curl, normals, scale, medium, lift,
         (in0, in1, in2, in3), emit,
     )
     for i in range(NF):
-        @pl.when(i < meta[NB])
-        def _():
-            copy(i).wait()
+        copy(i).wait()
 
 
 def fine_plan(levels):
@@ -417,7 +422,7 @@
             array(TAB, BLK),
             array(4 * FPAD, KROWS, dtype=BF16),
         ] + message(NB * BFB),
-        in_specs=[HBM] * 3,
+        in_specs=[VMEM] + [HBM] * 3,
         out_specs=[VMEM] * 7,
         scratch_shapes=[
             pltpu.VMEM((6, NPAD, NB * BLK), F32),
@@ -431,7 +436,7 @@
         compiler_params=PARAMS,
         cost_estimate=cost(10**9, 2 * 10**6),
         name="border",
-    )(codes, fields, face_interp.transpose(1, 0, 2))
+    )(ranks, codes, fields, face_interp.transpose(1, 0, 2))
     received = exchange(out)
     meta, outer, curl, rows, send, place, back, lift_wide = pl.pallas_call(
         volume_kernel,
@@ -457,34 +462,46 @@
         name="volume",
     )(neighbor.reshape(SLOTS), ranks, codes, slots, table, fields, metric, derivative, lift)
     rows = rows.reshape(FSLOTS)
-    rate, start, table, *out = pl.pallas_call(
+    geometry = (normals, face_scale, medium)
+    all_table, all_curl = table, curl
+    start, state, table, *out, all_outer = pl.pallas_call(
         full_kernel,
-        out_shape=[array(6, NP, NB * BLK), state_shape, array(FTAB, BLK)] + message(NF * BFB) + [array(SLOTS, BLK)],
+        out_shape=[state_shape] * 2 + [array(FTAB, BLK)] + message(NF * BFB) + [array(SLOTS, BLK)],
         in_specs=[SMEM] * 3 + [VMEM] * 12,
-        out_specs=[HBM] + [VMEM] * 7,
-        scratch_shapes=[
-            pltpu.VMEM((NB, 6, NP, BLK), F32),
-            pltpu.VMEM((NB, 6, NPAD, BLK), F32),
-            pltpu.SemaphoreType.DMA((NB,)),
-        ],
+        out_specs=[VMEM] * 8,
         input_output_aliases={4: 7},
         compiler_params=PARAMS,
         cost_estimate=cost(10**9, 4 * 10**6),
         name="full",
-    )(slots, send, meta, table, outer, curl, normals, face_scale, medium, front, lift_wide, *received)
-    state = start
+    )(slots, send, meta, all_table, outer, curl, *geometry, front, lift_wide, *received)
     for step in range(3):
         received = exchange(out)
-        outer, curl = pl.pallas_call(
-            fine_volume_kernel,
-            out_shape=[array(FSLOTS + 8, BLK), state_shape],
-            in_specs=[SMEM] * 2 + [VMEM] * 4,
-            out_specs=[VMEM] * 2,
-            compiler_params=PARAMS,
-            cost_estimate=cost(10**9, 2 * 10**6),
-            name="fine_volume",
-        )(rows, meta, table, state, metric, back)
-        geometry = (normals, face_scale, medium)
+        volume_shape = [array(FSLOTS + 8, BLK), state_shape]
+        volume_args = (rows, meta, table, state, metric, back)
+        if step == 0:
+            outer, curl, rate = pl.pallas_call(
+                coarse_kernel,
+                out_shape=volume_shape + [array(6, NP, NB * BLK)],
+                in_specs=[SMEM] * 2 + [VMEM] * 11,
+                out_specs=[VMEM] * 2 + [HBM],
+                scratch_shapes=[
+                    pltpu.VMEM((NB - NF, 6, NP, BLK), F32),
+                    pltpu.SemaphoreType.DMA((NB - NF,)),
+                ],
+                compiler_params=PARAMS,
+                cost_estimate=cost(10**9, 2 * 10**6),
+                name="coarse",
+            )(*volume_args, all_outer, all_table, all_curl, *geometry, lift_wide)
+        else:
+            outer, curl = pl.pallas_call(
+                fine_volume_kernel,
+                out_shape=volume_shape,
+                in_specs=[SMEM] * 2 + [VMEM] * 4,
+                out_specs=[VMEM] * 2,
+                compiler_params=PARAMS,
+                cost_estimate=cost(10**9, 2 * 10**6),
+                name="fine_volume",
+            )(*volume_args)
         if step < 2:
             state, table, *out = pl.pallas_call(
                 fine_kernel,

time: 95 us -> 93.3 us (0.982)
  starting transfers between devices: 55.9 us -> 54.9 us
    unnamed x24 -> x18, local copies, waits for them, and re-layouts: 3.9 us -> 2.7 us
    ppermute x4, starting transfers between devices: 19.8 us -> 18.8 us  [exchange(): lax.ppermute(out[3], 'py', y_up)]
  transfers between devices with their start and end apart: 16 -> 16, of which waited for: 3 -> 4; matrix products, arithmetic and copies ran while one was open for 1% -> 0% of each run, Pallas kernels for 11% -> 13%
where the time goes in v2:
time: 93.3 us; the launch traced here: 91.8 us
  starting transfers between devices  54.9 us (59%)
  Pallas kernels  24.2 us (26%)
  waiting for transfers between devices  7.91 us (8%)
  local copies, waits for them, and re-layouts  3.79 us (4%)
    ppermute x4, starting transfers between devices, exchange(): lax.ppermute(out[0], 'px', x_down)  23 us
    ppermute x4, starting transfers between devices, exchange(): lax.ppermute(out[3], 'py', y_up)  18.8 us
    ppermute x4, waiting for transfers between devices, exchange(): lax.ppermute(out[2], 'py', y_down)  7.88 us
    ppermute x4, starting transfers between devices, exchange(): lax.ppermute(out[1], 'px', x_up)  7.68 us
    ppermute x4, starting transfers between devices, exchange(): lax.ppermute(out[2], 'py', y_down)  5.35 us
    pallas_call x2, Pallas kernels, shards(): pl.pallas_call(fine_kernel, out_shape=[state_shape, array(FTAB, BLK)] + m...  4.57 us
    pallas_call x1, Pallas kernels, shards(): pl.pallas_call(volume_kernel, out_shape=[array(NB + 1, dtype=jnp.int32),...  4.18 us
    pallas_call x2, Pallas kernels, shards(): pl.pallas_call(fine_volume_kernel, out_shape=volume_shape, in_specs=[SMEM...  4.12 us
  transfers between devices with their start and end apart: 16, of which 4 were waited for; matrix products, arithmetic and copies ran while one was open for 0% of the time, Pallas kernels for 13%

profile of v2, /device:TPU:6, one launch (start us, length us, event | category | flops | bytes accessed | tf_op | source)
XLA Modules:
  0.0 91.8 jit_solution(3556202189147798677)
XLA Ops:
  4.3 2.4 %border.1 = (s32[8,128]{1,0:T(8,128)S(1)}, f32[4608,128]{1,0:T(8,128)S(1)}, bf16[64,128]{1,0:T(8,128)(2,1)S(1)}, f32[128,128]{1,0:T(8,128)S(1)}, f32[128,128]{1,...) custom-call(s32[6,8]{1,0:T(8,128)S(1)} %pad_add_fusion.ranks.rank, s32[32,128]{1,0:T(8,128)S(1)} %bitcast.19, ...), custom_call_target="tpu_custom_call" | custom-call | flops 1000000000 | bytes 2000000 | tf_op jit(solution)/shard_map/border/pallas_call | solution.py:418
  6.7 1.9 %collective-permute-start = (f32[128,128]{1,0:T(8,128)S(1)}, f32[128,128]{1,0:T(8,128)S(1)}, u32[]{:S(2)}, u32[]{:S(2)}) collective-permute-start(f32[128,128]{1,0:T(8,128)S(1)} %get-tuple-element.57), channel_id=1, source_target_pairs={{0,12},{12,24},{24,36},{36,48},{48,60},{60,72},{72,84},{84,96},{96... | collective-permute-start | bytes 196616 | tf_op jit(solution)/shard_map/ppermute | solution.py:404
  8.6 5.8 %collective-permute-start.1 = (f32[128,128]{1,0:T(8,128)S(1)}, f32[128,128]{1,0:T(8,128)S(1)}, u32[]{:S(2)}, u32[]{:S(2)}) collective-permute-start(f32[128,128]{1,0:T(8,128)S(1)} %get-tuple-element.58), channel_id=1, source_target_pairs={{12,0},{24,12},{36,24},{48,36},{60,48},{72,60},{84,72},{96,84},{10... | collective-permute-start | bytes 196616 | tf_op jit(solution)/shard_map/ppermute | solution.py:405
  14.4 4.3 %collective-permute-start.2 = (f32[128,128]{1,0:T(8,128)S(1)}, f32[128,128]{1,0:T(8,128)S(1)}, u32[]{:S(2)}, u32[]{:S(2)}) collective-permute-start(f32[128,128]{1,0:T(8,128)S(1)} %get-tuple-element.59), channel_id=1, source_target_pairs={{0,1},{1,2},{2,3},{3,4},{4,5},{5,6},{6,7},{7,8},{8,9},{9,10},{10,1... | collective-permute-start | bytes 196616 | tf_op jit(solution)/shard_map/ppermute | solution.py:406
  20.0 4.2 %volume.1 = (s32[9]{0:T(128)S(1)}, f32[4096,128]{1,0:T(8,128)S(1)}, f32[8,6,40,128]{3,2,1,0:T(8,128)S(1)}, s32[16,128]{1,0:T(8,128)S(1)}, s32[4,128]{1,0:T(4,128...) custom-call(s32[4096]{0:T(1024)S(1)} %bitcast.20, ...), custom_call_target="tpu_custom_call" | custom-call | flops 1000000000 | bytes 4000000 | tf_op jit(solution)/shard_map/volume/pallas_call | solution.py:441
  25.2 2.3 %full.1 = (f32[4,6,40,128]{3,2,1,0:T(8,128)S(1)}, f32[4,6,40,128]{3,2,1,0:T(8,128)S(1)}, f32[2056,128]{1,0:T(8,128)S(1)}, f32[64,128]{1,0:T(8,128)S(1)}, f32[64,...) custom-call(s32[8,128]{1,0:T(8,128)S(1)} %get-tuple-element.48.slots, ...), custom_call_target="tpu_custom_call", output_to_operand_aliasing={{7}: (4, {})} | custom-call | flops 1000000000 | bytes 4000000 | tf_op jit(solution)/shard_map/full/pallas_call | solution.py:467
  27.5 1.9 %collective-permute-start.4 = (f32[64,128]{1,0:T(8,128)S(1)}, f32[64,128]{1,0:T(8,128)S(1)}, u32[]{:S(2)}, u32[]{:S(2)}) collective-permute-start(f32[64,128]{1,0:T(8,128)S(1)} %get-tuple-element.69), channel_id=1, source_target_pairs={{0,12},{12,24},{24,36},{36,48},{48,60},{60,72},{72,84},{84,96},{96... | collective-permute-start | bytes 98312 | tf_op jit(solution)/shard_map/ppermute | solution.py:404
  29.4 5.8 %collective-permute-start.5 = (f32[64,128]{1,0:T(8,128)S(1)}, f32[64,128]{1,0:T(8,128)S(1)}, u32[]{:S(2)}, u32[]{:S(2)}) collective-permute-start(f32[64,128]{1,0:T(8,128)S(1)} %get-tuple-element.70), channel_id=1, source_target_pairs={{12,0},{24,12},{36,24},{48,36},{60,48},{72,60},{84,72},{96,84},{10... | collective-permute-start | bytes 98312 | tf_op jit(solution)/shard_map/ppermute | solution.py:405
  35.2 4.3 %collective-permute-start.6 = (f32[64,128]{1,0:T(8,128)S(1)}, f32[64,128]{1,0:T(8,128)S(1)}, u32[]{:S(2)}, u32[]{:S(2)}) collective-permute-start(f32[64,128]{1,0:T(8,128)S(1)} %get-tuple-element.71), channel_id=1, source_target_pairs={{0,1},{1,2},{2,3},{3,4},{4,5},{5,6},{6,7},{7,8},{8,9},{9,10},{10,1... | collective-permute-start | bytes 98312 | tf_op jit(solution)/shard_map/ppermute | solution.py:406
  40.8 3.8 %coarse.1 = (f32[2056,128]{1,0:T(8,128)S(1)}, f32[4,6,40,128]{3,2,1,0:T(8,128)S(1)}, f32[6,35,1024]{2,1,0:T(8,128)}) custom-call(s32[2048]{0:T(1024)S(1)} %bitcast.15, s32[9]{0:T(128)S(1)} %get-tuple-element.51.meta, f32[2056,128]{1,0:T(8,128)S(1)} %get-tuple-element.63.table, f32[4,6,40,128]{3,2,1,0:T(8,128)S(1)} %get-tuple-element.61.state, ...), custom_call_target="tpu_custom_call" | custom-call | flops 1000000000 | bytes 2000000 | tf_op jit(solution)/shard_map/coarse/pallas_call | solution.py:482
  44.6 2.2 %collective-permute-done.7.in3 = f32[64,128]{1,0:T(8,128)S(1)} collective-permute-done((f32[64,128]{1,0:T(8,128)S(1)}, f32[64,128]{1,0:T(8,128)S(1)}, u32[]{:S(2)}, u32[]{:S(2)}) %collective-permute-start.7) | collective-permute-done | bytes 32800 | tf_op jit(solution)/shard_map/ppermute | solution.py:407
  46.9 2.3 %fine.2 = (f32[4,6,40,128]{3,2,1,0:T(8,128)S(1)}, f32[2056,128]{1,0:T(8,128)S(1)}, f32[64,128]{1,0:T(8,128)S(1)}, f32[64,128]{1,0:T(8,128)S(1)}, f32[64,128]{1,0...) custom-call(s32[16,128]{1,0:T(8,128)S(1)} %get-tuple-element.50.place, ...), custom_call_target="tpu_custom_call", output_to_operand_aliasing={{6}: (6, {})} | custom-call | flops 1000000000 | bytes 2000000 | tf_op jit(solution)/shard_map/fine/pallas_call | solution.py:506
  49.2 1.9 %collective-permute-start.8 = (f32[64,128]{1,0:T(8,128)S(1)}, f32[64,128]{1,0:T(8,128)S(1)}, u32[]{:S(2)}, u32[]{:S(2)}) collective-permute-start(f32[64,128]{1,0:T(8,128)S(1)} %get-tuple-element.77), channel_id=1, source_target_pairs={{0,12},{12,24},{24,36},{36,48},{48,60},{60,72},{72,84},{84,96},{96... | collective-permute-start | bytes 98312 | tf_op jit(solution)/shard_map/ppermute | solution.py:404
  51.1 5.8 %collective-permute-start.9 = (f32[64,128]{1,0:T(8,128)S(1)}, f32[64,128]{1,0:T(8,128)S(1)}, u32[]{:S(2)}, u32[]{:S(2)}) collective-permute-start(f32[64,128]{1,0:T(8,128)S(1)} %get-tuple-element.78), channel_id=1, source_target_pairs={{12,0},{24,12},{36,24},{48,36},{60,48},{72,60},{84,72},{96,84},{10... | collective-permute-start | bytes 98312 | tf_op jit(solution)/shard_map/ppermute | solution.py:405
  56.8 5.1 %collective-permute-start.10 = (f32[64,128]{1,0:T(8,128)S(1)}, f32[64,128]{1,0:T(8,128)S(1)}, u32[]{:S(2)}, u32[]{:S(2)}) collective-permute-start(f32[64,128]{1,0:T(8,128)S(1)} %get-tuple-element.79), channel_id=1, source_target_pairs={{0,1},{1,2},{2,3},{3,4},{4,5},{5,6},{6,7},{7,8},{8,9},{9,10},{10,1... | collective-permute-start | bytes 98312 | tf_op jit(solution)/shard_map/ppermute | solution.py:406
  63.5 2.1 %fine_volume.2 = (f32[2056,128]{1,0:T(8,128)S(1)}, f32[4,6,40,128]{3,2,1,0:T(8,128)S(1)}) custom-call(s32[2048]{0:T(1024)S(1)} %bitcast.16, s32[9]{0:T(128)S(1)} %get-tuple-element.51.meta, f32[2056,128]{1,0:T(8,128)S(1)} %get-tuple-element.74.table, f32[4,6,40,128]{3,2,1,0:T(8,128)S(1)} %get-tuple-element.73.state, f32[3,3,1024]{2,1,0:T(4,128)S(1)} %copy-done.3, ...), custom_call_target="tpu_custom_call" | custom-call | flops 1000000000 | bytes 2000000 | tf_op jit(solution)/shard_map/fine_volume/pallas_call | solution.py:496
  65.6 2.3 %collective-permute-done.11.in3 = f32[64,128]{1,0:T(8,128)S(1)} collective-permute-done((f32[64,128]{1,0:T(8,128)S(1)}, f32[64,128]{1,0:T(8,128)S(1)}, u32[]{:S(2)}, u32[]{:S(2)}) %collective-permute-start.11) | collective-permute-done | bytes 32800 | tf_op jit(solution)/shard_map/ppermute | solution.py:407
  67.9 2.3 %fine.3 = (f32[4,6,40,128]{3,2,1,0:T(8,128)S(1)}, f32[2056,128]{1,0:T(8,128)S(1)}, f32[64,128]{1,0:T(8,128)S(1)}, f32[64,128]{1,0:T(8,128)S(1)}, f32[64,128]{1,0...) custom-call(s32[16,128]{1,0:T(8,128)S(1)} %get-tuple-element.50.place, ...), custom_call_target="tpu_custom_call", output_to_operand_aliasing={{6}: (6, {})} | custom-call | flops 1000000000 | bytes 2000000 | tf_op jit(solution)/shard_map/fine/pallas_call | solution.py:506
  70.2 1.9 %collective-permute-start.12 = (f32[64,128]{1,0:T(8,128)S(1)}, f32[64,128]{1,0:T(8,128)S(1)}, u32[]{:S(2)}, u32[]{:S(2)}) collective-permute-start(f32[64,128]{1,0:T(8,128)S(1)} %get-tuple-element.85), channel_id=1, source_target_pairs={{0,12},{12,24},{24,36},{36,48},{48,60},{60,72},{72,84},{84,96},{96... | collective-permute-start | bytes 98312 | tf_op jit(solution)/shard_map/ppermute | solution.py:404
  72.1 5.8 %collective-permute-start.13 = (f32[64,128]{1,0:T(8,128)S(1)}, f32[64,128]{1,0:T(8,128)S(1)}, u32[]{:S(2)}, u32[]{:S(2)}) collective-permute-start(f32[64,128]{1,0:T(8,128)S(1)} %get-tuple-element.86), channel_id=1, source_target_pairs={{12,0},{24,12},{36,24},{48,36},{60,48},{72,60},{84,72},{96,84},{10... | collective-permute-start | bytes 98312 | tf_op jit(solution)/shard_map/ppermute | solution.py:405
  77.9 5.1 %collective-permute-start.14 = (f32[64,128]{1,0:T(8,128)S(1)}, f32[64,128]{1,0:T(8,128)S(1)}, u32[]{:S(2)}, u32[]{:S(2)}) collective-permute-start(f32[64,128]{1,0:T(8,128)S(1)} %get-tuple-element.87), channel_id=1, source_target_pairs={{0,1},{1,2},{2,3},{3,4},{4,5},{5,6},{6,7},{7,8},{8,9},{9,10},{10,1... | collective-permute-start | bytes 98312 | tf_op jit(solution)/shard_map/ppermute | solution.py:406
  84.3 2.1 %fine_volume.3 = (f32[2056,128]{1,0:T(8,128)S(1)}, f32[4,6,40,128]{3,2,1,0:T(8,128)S(1)}) custom-call(s32[2048]{0:T(1024)S(1)} %bitcast.17, s32[9]{0:T(128)S(1)} %get-tuple-element.51.meta, f32[2056,128]{1,0:T(8,128)S(1)} %get-tuple-element.82.table, f32[4,6,40,128]{3,2,1,0:T(8,128)S(1)} %get-tuple-element.81.state, f32[3,3,1024]{2,1,0:T(4,128)S(1)} %copy-done.3, ...), custom_call_target="tpu_custom_call" | custom-call | flops 1000000000 | bytes 2000000 | tf_op jit(solution)/shard_map/fine_volume/pallas_call | solution.py:496
  86.4 2.4 %collective-permute-done.15.in3 = f32[64,128]{1,0:T(8,128)S(1)} collective-permute-done((f32[64,128]{1,0:T(8,128)S(1)}, f32[64,128]{1,0:T(8,128)S(1)}, u32[]{:S(2)}, u32[]{:S(2)}) %collective-permute-start.15) | collective-permute-done | bytes 32800 | tf_op jit(solution)/shard_map/ppermute | solution.py:407
  88.8 2.8 %last.1 = (f32[6,35,1024]{2,1,0:T(8,128)}, f32[2056,128]{1,0:T(8,128)S(1)}) custom-call(s32[16,128]{1,0:T(8,128)S(1)} %get-tuple-element.50.place, s32[9]{0:T(128)S(1)} %get-tuple-element.51.meta, f32[4,6,40,128]{3,2,1,0:T(8,128)S(1)} %get-tuple-element.81.state, ...), custom_call_target="tpu_custom_call", output_to_operand_aliasing={{0}: (15, {}), {1}: (5, {})} | custom-call | flops 1000000000 | bytes 2000000 | tf_op jit(solution)/shard_map/last/pallas_call | solution.py:516
  (45 shorter events, 10.6 us)
Async XLA Ops:
  1.6 1.2 %copy-start.4 = (f32[6,35,1024]{2,1,0:T(8,128)S(1)}, f32[6,35,1024]{2,1,0:T(8,128)}, u32[]{:S(2)}) copy-start(f32[6,35,1024]{2,1,0:T(8,128)} %fields.3) | copy-start | bytes 2580484
  2.8 0.8 copy-start.6
  4.3 15.7 %copy-start.3 = (f32[3,3,1024]{2,1,0:T(4,128)S(1)}, f32[3,3,1024]{2,1,0:T(4,128)}, u32[]{:S(2)}) copy-start(f32[3,3,1024]{2,1,0:T(4,128)} %metric.7) | copy-start | bytes 110596
  4.3 15.7 %copy-start.5 = (f32[3,35,35]{2,1,0:T(8,128)S(1)}, f32[3,35,35]{2,1,0:T(8,128)}, u32[]{:S(2)}) copy-start(f32[3,35,35]{2,1,0:T(8,128)} %derivative.1) | copy-start | bytes 44104
  4.3 15.7 %copy-start.7 = (f32[35,60]{1,0:T(8,128)S(1)}, f32[35,60]{1,0:T(8,128)}, u32[]{:S(2)}) copy-start(f32[35,60]{1,0:T(8,128)} %lift.1) | copy-start | bytes 25204
  6.7 17.5 %collective-permute-start = (f32[128,128]{1,0:T(8,128)S(1)}, f32[128,128]{1,0:T(8,128)S(1)}, u32[]{:S(2)}, u32[]{:S(2)}) collective-permute-start(f32[128,128]{1,0:T(8,128)S(1)} %get-tuple-element.57), channel_id=1, source_target_pairs={{0,12},{12,24},{24,36},{36,48},{48,60},{60,72},{72,84},{84,96},{96... | collective-permute-start | bytes 196616 | tf_op jit(solution)/shard_map/ppermute | solution.py:404
  8.6 15.6 %collective-permute-start.1 = (f32[128,128]{1,0:T(8,128)S(1)}, f32[128,128]{1,0:T(8,128)S(1)}, u32[]{:S(2)}, u32[]{:S(2)}) collective-permute-start(f32[128,128]{1,0:T(8,128)S(1)} %get-tuple-element.58), channel_id=1, source_target_pairs={{12,0},{24,12},{36,24},{48,36},{60,48},{72,60},{84,72},{96,84},{10... | collective-permute-start | bytes 196616 | tf_op jit(solution)/shard_map/ppermute | solution.py:405
  14.4 9.9 %collective-permute-start.2 = (f32[128,128]{1,0:T(8,128)S(1)}, f32[128,128]{1,0:T(8,128)S(1)}, u32[]{:S(2)}, u32[]{:S(2)}) collective-permute-start(f32[128,128]{1,0:T(8,128)S(1)} %get-tuple-element.59), channel_id=1, source_target_pairs={{0,1},{1,2},{2,3},{3,4},{4,5},{5,6},{6,7},{7,8},{8,9},{9,10},{10,1... | collective-permute-start | bytes 196616 | tf_op jit(solution)/shard_map/ppermute | solution.py:406
  18.7 6.5 %collective-permute-start.3 = (f32[128,128]{1,0:T(8,128)S(1)}, f32[128,128]{1,0:T(8,128)S(1)}, u32[]{:S(2)}, u32[]{:S(2)}) collective-permute-start(f32[128,128]{1,0:T(8,128)S(1)} %get-tuple-element.60), channel_id=1, source_target_pairs={{1,0},{2,1},{3,2},{4,3},{5,4},{6,5},{7,6},{8,7},{9,8},{10,9},{11,1... | collective-permute-start | bytes 196616 | tf_op jit(solution)/shard_map/ppermute | solution.py:407
  20.0 5.2 %copy-start = (f32[3,4,1024]{2,1,0:T(4,128)S(1)}, f32[3,4,1024]{2,1,0:T(4,128)}, u32[]{:S(2)}) copy-start(f32[3,4,1024]{2,1,0:T(4,128)} %normals.9) | copy-start | bytes 147460
  20.0 5.2 %copy-start.1 = (f32[4,1024]{1,0:T(4,128)S(1)}, f32[4,1024]{1,0:T(4,128)}, u32[]{:S(2)}) copy-start(f32[4,1024]{1,0:T(4,128)} %scale.9) | copy-start | bytes 49156
  20.0 5.2 %copy-start.2 = (f32[1024]{0:T(1024)S(1)}, f32[1024]{0:T(1024)}, u32[]{:S(2)}) copy-start(f32[1024]{0:T(1024)} %param.14) | copy-start | bytes 12292
  27.5 17.1 %collective-permute-start.4 = (f32[64,128]{1,0:T(8,128)S(1)}, f32[64,128]{1,0:T(8,128)S(1)}, u32[]{:S(2)}, u32[]{:S(2)}) collective-permute-start(f32[64,128]{1,0:T(8,128)S(1)} %get-tuple-element.69), channel_id=1, source_target_pairs={{0,12},{12,24},{24,36},{36,48},{48,60},{60,72},{72,84},{84,96},{96... | collective-permute-start | bytes 98312 | tf_op jit(solution)/shard_map/ppermute | solution.py:404
  29.4 15.2 %collective-permute-start.5 = (f32[64,128]{1,0:T(8,128)S(1)}, f32[64,128]{1,0:T(8,128)S(1)}, u32[]{:S(2)}, u32[]{:S(2)}) collective-permute-start(f32[64,128]{1,0:T(8,128)S(1)} %get-tuple-element.70), channel_id=1, source_target_pairs={{12,0},{24,12},{36,24},{48,36},{60,48},{72,60},{84,72},{96,84},{10... | collective-permute-start | bytes 98312 | tf_op jit(solution)/shard_map/ppermute | solution.py:405
  35.2 9.4 %collective-permute-start.6 = (f32[64,128]{1,0:T(8,128)S(1)}, f32[64,128]{1,0:T(8,128)S(1)}, u32[]{:S(2)}, u32[]{:S(2)}) collective-permute-start(f32[64,128]{1,0:T(8,128)S(1)} %get-tuple-element.71), channel_id=1, source_target_pairs={{0,1},{1,2},{2,3},{3,4},{4,5},{5,6},{6,7},{7,8},{8,9},{9,10},{10,1... | collective-permute-start | bytes 98312 | tf_op jit(solution)/shard_map/ppermute | solution.py:406
  39.5 7.4 %collective-permute-start.7 = (f32[64,128]{1,0:T(8,128)S(1)}, f32[64,128]{1,0:T(8,128)S(1)}, u32[]{:S(2)}, u32[]{:S(2)}) collective-permute-start(f32[64,128]{1,0:T(8,128)S(1)} %get-tuple-element.72), channel_id=1, source_target_pairs={{1,0},{2,1},{3,2},{4,3},{5,4},{6,5},{7,6},{8,7},{9,8},{10,9},{11,1... | collective-permute-start | bytes 98312 | tf_op jit(solution)/shard_map/ppermute | solution.py:407
  49.2 16.4 %collective-permute-start.8 = (f32[64,128]{1,0:T(8,128)S(1)}, f32[64,128]{1,0:T(8,128)S(1)}, u32[]{:S(2)}, u32[]{:S(2)}) collective-permute-start(f32[64,128]{1,0:T(8,128)S(1)} %get-tuple-element.77), channel_id=1, source_target_pairs={{0,12},{12,24},{24,36},{36,48},{48,60},{60,72},{72,84},{84,96},{96... | collective-permute-start | bytes 98312 | tf_op jit(solution)/shard_map/ppermute | solution.py:404
  51.1 14.5 %collective-permute-start.9 = (f32[64,128]{1,0:T(8,128)S(1)}, f32[64,128]{1,0:T(8,128)S(1)}, u32[]{:S(2)}, u32[]{:S(2)}) collective-permute-start(f32[64,128]{1,0:T(8,128)S(1)} %get-tuple-element.78), channel_id=1, source_target_pairs={{12,0},{24,12},{36,24},{48,36},{60,48},{72,60},{84,72},{96,84},{10... | collective-permute-start | bytes 98312 | tf_op jit(solution)/shard_map/ppermute | solution.py:405
  56.8 8.7 %collective-permute-start.10 = (f32[64,128]{1,0:T(8,128)S(1)}, f32[64,128]{1,0:T(8,128)S(1)}, u32[]{:S(2)}, u32[]{:S(2)}) collective-permute-start(f32[64,128]{1,0:T(8,128)S(1)} %get-tuple-element.79), channel_id=1, source_target_pairs={{0,1},{1,2},{2,3},{3,4},{4,5},{5,6},{6,7},{7,8},{8,9},{9,10},{10,1... | collective-permute-start | bytes 98312 | tf_op jit(solution)/shard_map/ppermute | solution.py:406
  62.0 5.9 %collective-permute-start.11 = (f32[64,128]{1,0:T(8,128)S(1)}, f32[64,128]{1,0:T(8,128)S(1)}, u32[]{:S(2)}, u32[]{:S(2)}) collective-permute-start(f32[64,128]{1,0:T(8,128)S(1)} %get-tuple-element.80), channel_id=1, source_target_pairs={{1,0},{2,1},{3,2},{4,3},{5,4},{6,5},{7,6},{8,7},{9,8},{10,9},{11,1... | collective-permute-start | bytes 98312 | tf_op jit(solution)/shard_map/ppermute | solution.py:407
  70.2 16.2 %collective-permute-start.12 = (f32[64,128]{1,0:T(8,128)S(1)}, f32[64,128]{1,0:T(8,128)S(1)}, u32[]{:S(2)}, u32[]{:S(2)}) collective-permute-start(f32[64,128]{1,0:T(8,128)S(1)} %get-tuple-element.85), channel_id=1, source_target_pairs={{0,12},{12,24},{24,36},{36,48},{48,60},{60,72},{72,84},{84,96},{96... | collective-permute-start | bytes 98312 | tf_op jit(solution)/shard_map/ppermute | solution.py:404
  72.1 14.3 %collective-permute-start.13 = (f32[64,128]{1,0:T(8,128)S(1)}, f32[64,128]{1,0:T(8,128)S(1)}, u32[]{:S(2)}, u32[]{:S(2)}) collective-permute-start(f32[64,128]{1,0:T(8,128)S(1)} %get-tuple-element.86), channel_id=1, source_target_pairs={{12,0},{24,12},{36,24},{48,36},{60,48},{72,60},{84,72},{96,84},{10... | collective-permute-start | bytes 98312 | tf_op jit(solution)/shard_map/ppermute | solution.py:405
  77.9 8.5 %collective-permute-start.14 = (f32[64,128]{1,0:T(8,128)S(1)}, f32[64,128]{1,0:T(8,128)S(1)}, u32[]{:S(2)}, u32[]{:S(2)}) collective-permute-start(f32[64,128]{1,0:T(8,128)S(1)} %get-tuple-element.87), channel_id=1, source_target_pairs={{0,1},{1,2},{2,3},{3,4},{4,5},{5,6},{6,7},{7,8},{8,9},{9,10},{10,1... | collective-permute-start | bytes 98312 | tf_op jit(solution)/shard_map/ppermute | solution.py:406
  83.0 5.8 %collective-permute-start.15 = (f32[64,128]{1,0:T(8,128)S(1)}, f32[64,128]{1,0:T(8,128)S(1)}, u32[]{:S(2)}, u32[]{:S(2)}) collective-permute-start(f32[64,128]{1,0:T(8,128)S(1)} %get-tuple-element.88), channel_id=1, source_target_pairs={{1,0},{2,1},{3,2},{4,3},{5,4},{6,5},{7,6},{8,7},{9,8},{10,9},{11,1... | collective-permute-start | bytes 98312 | tf_op jit(solution)/shard_map/ppermute | solution.py:407
  (1 other events, 0.7 us)
